TPU v7x, 32 devices: a whole 2x2x4 slice. The times are simulated.
32 devices in a mesh: teacher: 4 (over y, x), dp: 8 (over z, core).
Axes of the slice: x: 2, y: 2, z: 4, core: 2. Of those that a mesh axis runs over, the one named last changes fastest.
Arguments:
- hid_whisper: bfloat16 [4096, 1280], P(('teacher', 'dp')), may hold values from -6 to 6
- hid_beats: bfloat16 [4096, 768], P(('teacher', 'dp')), may hold values from -6 to 6
- hid_wavlm: bfloat16 [4096, 1024], P(('teacher', 'dp')), may hold values from -6 to 6
- up_whisper: bfloat16 [1280, 5120], P(None, 'teacher'), may hold values from -0.15625 to 0.15625
- down_whisper: bfloat16 [5120, 1280], P('teacher'), may hold values from -0.078125 to 0.078125
- up_beats: bfloat16 [768, 3072], P(None, 'teacher'), may hold values from -0.21875 to 0.21875
- down_beats: bfloat16 [3072, 768], P('teacher'), may hold values from -0.109375 to 0.109375
- up_wavlm: bfloat16 [1024, 4096], P(None, 'teacher'), may hold values from -0.1875 to 0.1875
- down_wavlm: bfloat16 [4096, 1024], P('teacher'), may hold values from -0.09375 to 0.09375
- clip_len: int32 [32], P(('teacher', 'dp')), may hold values from 16 to 128
- send_counts: int32 [4, 8, 8], P('teacher'), may hold values from 0 to 32, as said below
- student_in: bfloat16 [4096, 512], P(('teacher', 'dp')), may hold values from -6 to 6
- w_in: bfloat16 [512, 1536], P('dp'), may hold values from -0.25 to 0.25
- w_out: bfloat16 [1536, 512], P('dp'), may hold values from -0.15625 to 0.15625
- w_head: bfloat16 [512, 3072], P('dp'), may hold values from -0.25 to 0.25
Outputs:
- grad_in: float32 [512, 1536], P('dp')
- grad_out: float32 [1536, 512], P('dp')
- grad_head: float32 [512, 3072], P('dp')
Inputs may be any that keep to these rules, and one draw needn't show every extreme that they name: In every group t, each source s hands 128 frames in all (the sum over o of send_counts[t,s,o]), each owner o receives 128 frames in all, and in every group some source hands exactly 32 frames to some owner.
All inputs are finite; a program needn't handle non-finite values.
Results may differ from a plain program's by a relative error of at most 0.0031.
Values may be sent and summed in bfloat16 or wider, within the bound.
No kernel may reach another device: no remote copies, remote signals or barrier semaphores. Data moves between devices by JAX's collectives and lax.ppermute only.
A program may use at most 128 MiB of HBM per device.

v0:
```python
import functools

import jax
import jax.numpy as jnp
from jax import lax
from jax.experimental import pallas as pl
from jax.experimental.pallas import tpu as pltpu
from jax.sharding import PartitionSpec as P

EPS = 1e-05
BF = jnp.bfloat16
F32 = jnp.float32
I32 = jnp.int32
BLK = 256
FFN_MB = 50
VMEM = pl.BlockSpec(memory_space=pltpu.VMEM)
SMEM = pl.BlockSpec(memory_space=pltpu.SMEM)
ANY = pl.BlockSpec(memory_space=pl.ANY)
HBM = pl.BlockSpec(memory_space=pltpu.HBM)


def dot(a, b, dims=((1,), (0,))):
    return lax.dot_general(a, b, (dims, ((), ())), preferred_element_type=F32)


def layer_norm(values):
    wide = values.astype(F32)
    center = wide - jnp.mean(wide, axis=-1, keepdims=True)
    spread = jnp.mean(center * center, axis=-1, keepdims=True)
    return center * lax.rsqrt(spread + EPS)


def gelu(x):
    return 0.5 * x * (1.0 + lax.erf(x * 0.7071067811865476))


def aligned(index, size, to):
    return pl.ds(pl.multiple_of(index * size, to), size)


def call(kernel, name, out_shape, in_specs, scratch=(), out_specs=None, limit=8, us=1):
    many = isinstance(out_shape, (list, tuple))
    if out_specs is None:
        out_specs = [VMEM] * len(out_shape) if many else VMEM
    return pl.pallas_call(
        kernel,
        out_shape=out_shape,
        in_specs=in_specs,
        out_specs=out_specs,
        scratch_shapes=list(scratch),
        name=name,
        cost_estimate=pl.CostEstimate(flops=int(us * 1e9), bytes_accessed=int(us * 3e6), transcendentals=0),
        compiler_params=pltpu.CompilerParams(vmem_limit_bytes=limit * 1024 * 1024),
    )


def shape(dims, dtype):
    return jax.ShapeDtypeStruct(dims, dtype)


def pack_kernel(n_t, n_dp, cap, table, student, w_head, out):
    me = lax.axis_index("dp")
    frames, sd = student.shape
    rows = 2 * cap
    row = lax.broadcasted_iota(I32, (n_dp * rows, frames), 0)
    col = lax.broadcasted_iota(I32, (n_dp * rows, frames), 1)
    start = jnp.zeros((n_dp * rows, frames), I32)
    running = jnp.int32(0)
    for s in range(n_dp):
        start = jnp.where(row // rows == s, running, start)
        running = running + table[0, s, me]
    pick = (col == start + row % cap).astype(F32).astype(BF)
    half = sd // 2
    left, right = dot(pick, student[:, :half]), dot(pick, student[:, half:])
    first = lax.broadcasted_iota(I32, left.shape, 0) % rows < cap
    out[:, :half] = jnp.where(first, left, right).astype(BF)
    slice_w = w_head.shape[1] // n_t
    mine = w_head[:, aligned(lax.axis_index("teacher"), slice_w, 128)]
    for d in range(n_dp):
        lane = d % 2 * (slice_w // 2)
        out[pl.ds(d * rows, rows), half:] = mine[:, lane : lane + slice_w // 2]


def unpack_kernel(n_dp, cap, table, clip_len, arrived, out, head):
    me = lax.axis_index("dp")
    copies, frames, wide = out.shape
    sd = wide - 128
    half = sd // 2
    rows = 2 * cap
    row = lax.broadcasted_iota(I32, (frames, n_dp * rows), 0)
    col = lax.broadcasted_iota(I32, (frames, n_dp * rows), 1)
    slot = jnp.zeros((frames, n_dp * rows), I32)
    running = jnp.int32(0)
    for o in range(n_dp):
        here = table[0, me, o]
        inside = (row >= running) & (row < running + here)
        slot = jnp.where(inside, o * rows + row - running, slot)
        running = running + here
    parts = [
        dot((col == slot + at).astype(F32).astype(BF), arrived[:, :half]).astype(BF) for at in (0, cap)
    ]
    clips = clip_len.shape[0]
    slots = frames // clips
    frame = lax.broadcasted_iota(I32, (frames, wide - sd), 0)
    valid = jnp.zeros((frames, wide - sd), F32)
    for c in range(clips):
        used = (frame // slots == c) & (frame % slots < clip_len[c])
        valid = jnp.where(used, 1.0, valid)
    for k in range(copies):
        out[k, :, :half] = parts[0]
        out[k, :, half:sd] = parts[1]
        out[k, :, sd:] = valid.astype(BF)
    head[...] = arrived[:, half:]


def copy_all(pairs, sem):
    copies = [pltpu.make_async_copy(a, b, sem.at[i]) for i, (a, b) in enumerate(pairs)]
    for c in copies:
        c.start()
    for c in copies:
        c.wait()


def merge_kernel(w_in, w_out, whisper, beats, wavlm, after, merged, hid, sem):
    rows, sff = w_in.shape
    sd = w_out.shape[1]
    pairs = [(w_in, merged.at[:, pl.ds(0, sff)])]
    for p in range(w_out.shape[0] // rows):
        pairs.append((w_out.at[pl.ds(p * rows, rows), :], merged.at[:, pl.ds(sff + p * sd, sd)]))
    at = 0
    for ref in (whisper, beats, wavlm):
        pairs.append((ref, hid.at[:, pl.ds(at, ref.shape[1])]))
        at += ref.shape[1]
    copy_all(pairs, sem)


def halves_kernel(from_x, from_y, to_y, to_x, sem):
    half = to_x.shape[0]
    copy_all([(from_x.at[pl.ds(half, half), :], to_y), (from_y.at[pl.ds(0, half), :], to_x)], sem)


def ffn_kernel(slice_w, n, *refs):
    h_refs, w_refs, after, e_refs = refs[:n], refs[n : n + 6], refs[n + 6], refs[n + 7 : n + 10]
    hid, w_bufs, e_bufs, normed, sem = refs[n + 10], refs[n + 11 : n + 17], e_refs, refs[n + 17], refs[n + 18]
    me = lax.axis_index("teacher")
    frames = hid.shape[0]
    half = frames // 2
    pairs = []
    at = 0
    for ref in h_refs:
        pairs.append((ref, hid.at[pl.ds(at, ref.shape[0]), :]))
        at += ref.shape[0]
    pairs += list(zip(w_refs, w_bufs))
    copies = [pltpu.make_async_copy(a, b, sem.at[i]) for i, (a, b) in enumerate(pairs)]
    for c in copies:
        c.start()
    for c in copies[:n]:
        c.wait()
    starts = []
    first = 0
    for e in e_bufs:
        starts.append(first)
        first += e.shape[1]
    for k in (0, 2, 1):
        up, down, e = w_bufs[2 * k], w_bufs[2 * k + 1], e_bufs[k]
        width = e.shape[1]
        normed[:, pl.ds(0, width)] = layer_norm(hid[:, pl.ds(starts[k], width)]).astype(BF)
        copies[n + 2 * k].wait()
        hidden = [gelu(dot(normed[pl.ds(r, half), pl.ds(0, width)], up[...])).astype(BF) for r in (0, half)]
        copies[n + 2 * k + 1].wait()
        for i, r in enumerate((0, half)):
            e[pl.ds(r, half), :] = -dot(hidden[i], down[...])
        for b in range(0, width, BLK):

            @pl.when(me == (starts[k] + b) // slice_w)
            def _(b=b, e=e, k=k):
                e[:, pl.ds(b, BLK)] -= hid[:, pl.ds(starts[k] + b, BLK)].astype(F32)


def ffn(pieces, weights, slice_w, after):
    frames = sum(p.shape[0] for p in pieces)
    wall = pieces[0].shape[1]
    widths = [w.shape[1] for w in weights[1::2]]
    n = len(pieces)
    return call(
        functools.partial(ffn_kernel, slice_w, n),
        "ffn",
        [shape((frames, w), F32) for w in widths],
        [HBM] * (n + 6) + [ANY],
        scratch=[pltpu.VMEM((frames, wall), BF)]
        + [pltpu.VMEM(w.shape, BF) for w in weights]
        + [pltpu.VMEM((frames, max(widths)), BF), pltpu.SemaphoreType.DMA((n + 6,))],
        limit=FFN_MB,
        us=13,
    )(*pieces, *weights, after)


def forward_kernel(dims, *refs):
    n_t, n_z, rows, out_rows, slice_w = dims
    s_ref, w_refs, h_refs, refs = refs[0], refs[1 : 1 + 2 * n_z], refs[1 + 2 * n_z : 3 + 2 * n_z], refs[3 + 2 * n_z + n_t - 1 :]
    e_refs, (act, slope, w_out, err, keep, send), (w_in, w_head, pred, sem) = refs[:3], refs[3:9], refs[9:]
    me_t = lax.axis_index("teacher")
    me_d = lax.axis_index("dp")
    z, core = me_d // 2, me_d % 2
    sd, sff = w_in.shape
    parts = out_rows // rows
    pairs = []
    for i in range(2 * n_z):
        shard = 2 * (z ^ (i // 2)) + (core if i % 2 == 0 else 1 - core)
        src = w_refs[i]
        pairs.append((src.at[:, pl.ds(0, sff)], w_in.at[aligned(shard, rows, 16), :]))
        for p in range(parts):
            at = pl.multiple_of(shard * out_rows + p * rows, 16)
            pairs.append((src.at[:, pl.ds(sff + p * sd, sd)], w_out.at[pl.ds(at, rows), :]))
    for c in range(2):
        pairs.append((h_refs[c], w_head.at[:, aligned(core if c == 0 else 1 - core, slice_w // 2, 128)]))
    copy_all(pairs, sem)
    order = [me_t ^ k for k in range(n_t)]
    student = jnp.concatenate([s_ref[k, :, pl.ds(0, sd)] for k in order], axis=0)
    mask = jnp.concatenate([s_ref[k, :, pl.ds(sd, 128)] for k in order], axis=0).astype(F32)
    total = student.astype(F32)
    for b in range(0, sff, BLK):
        pre = dot(student, w_in[:, pl.ds(b, BLK)])
        low = pre - 4.0
        small = jnp.exp(-jnp.abs(low))
        swoosh = jnp.maximum(low, 0.0) + jnp.log(1.0 + small) - 0.08 * pre - 0.035
        swoosh = swoosh.astype(BF)
        act[:, pl.ds(b, BLK)] = swoosh
        slope[:, pl.ds(b, BLK)] = jnp.where(low >= 0.0, 1.0, small) / (1.0 + small) - 0.08
        total = total + dot(swoosh, w_out[pl.ds(b, BLK), :])
    features = total.astype(BF)
    feat_t = features.T
    pred[...] = dot(features, w_head[...])

    at = 0
    for ref in e_refs:
        width = ref.shape[1]
        scale = (2.0 / width) * mask
        for b in range(0, width, BLK):
            col = at + b
            value = ref[:, pl.ds(b, BLK)]
            guess = pred[:, pl.ds(col % slice_w, BLK)]
            value = value + jnp.where(me_t == col // slice_w, guess, 0.0)
            value = jnp.concatenate([value[:, c : c + 128] * scale for c in range(0, BLK, 128)], axis=1).astype(BF)
            err[:, pl.ds(col, BLK)] = value
            product = dot(feat_t, value)
            for i in range(n_z):
                pair = product[2 * i * rows : 2 * (i + 1) * rows]
                low, high = pair[:rows], pair[rows:]
                keep[i, :, pl.ds(col, BLK)] = jnp.where(core == 0, low, high)
                send[i, :, pl.ds(col, BLK)] = jnp.where(core == 0, high, low).astype(BF)
        at += width


def forward(s_all, w_pieces, h_pieces, after, e_parts, n_z, rows, out_rows, slice_w, sff):
    n_t, frames, sd = s_all.shape
    frames, sd = n_t * frames, sd - 128
    wall = sum(e.shape[1] for e in e_parts)
    return call(
        functools.partial(forward_kernel, (n_t, n_z, rows, out_rows, slice_w)),
        "student_forward",
        [
            shape((frames, sff), BF),
            shape((frames, sff), F32),
            shape((sff, sd), BF),
            shape((frames, wall), BF),
            shape((n_z, rows, wall), F32),
            shape((n_z, rows, wall), BF),
        ],
        [VMEM] + [ANY] * (2 * n_z + 2 + n_t - 1) + [VMEM] * 3,
        scratch=[
            pltpu.VMEM((sd, sff), BF),
            pltpu.VMEM((sd, slice_w), BF),
            pltpu.VMEM((frames, slice_w), F32),
        ]
        + [pltpu.SemaphoreType.DMA((2 * n_z * (1 + out_rows // rows) + 2,))],
        limit=16,
        us=7,
    )(s_all, *w_pieces, *h_pieces, *after, *e_parts)


def backward_kernel(dims, *refs):
    n_t, n_z, rows, out_rows, slice_w = dims
    s_ref, h_refs = refs[0], refs[1 : 1 + 2 * n_t]
    err, act, slope, w_out, after, keep, send, w_head, student_t, sem = refs[1 + 2 * n_t :]
    me_t = lax.axis_index("teacher")
    me_d = lax.axis_index("dp")
    z, core = me_d // 2, me_d % 2
    copies = []
    for k in range(n_t):
        for c in range(2):
            at = (me_t ^ k) * slice_w + (core if c == 0 else 1 - core) * (slice_w // 2)
            dst = w_head.at[:, pl.ds(pl.multiple_of(at, 128), slice_w // 2)]
            copies.append(pltpu.make_async_copy(h_refs[2 * k + c], dst, sem.at[len(copies)]))
    for c in copies:
        c.start()
    sd = w_head.shape[0]
    student = jnp.concatenate([s_ref[me_t ^ k, :, pl.ds(0, sd)] for k in range(n_t)], axis=0)
    student_t[...] = student.T
    for c in copies:
        c.wait()
    fg = dot(err[...], w_head[...], ((1,), (1,))).astype(BF)
    sff = act.shape[1]
    block = sff // 4
    zs = block // (2 * out_rows)
    for b in range(4):
        part = dot(act[:, pl.ds(b * block, block)].T, fg)
        for i in range(zs):
            for p in range(out_rows // rows):
                at = 2 * i * out_rows + p * rows
                low, high = part[at : at + rows], part[at + out_rows : at + out_rows + rows]
                lanes = pl.ds(p * sd, sd)
                keep[b * zs + i, :, lanes] = jnp.where(core == 0, low, high)
                send[b * zs + i, :, lanes] = jnp.where(core == 0, high, low).astype(BF)
        back = dot(fg, w_out[pl.ds(b * block, block), :], ((1,), (1,)))
        pre_grad = (back * slope[:, pl.ds(b * block, block)]).astype(BF)
        part = dot(student_t[...], pre_grad)
        for i in range(n_z):
            low = part[2 * i * rows : (2 * i + 1) * rows]
            high = part[(2 * i + 1) * rows : (2 * i + 2) * rows]
            lanes = pl.ds(out_rows // rows * sd + b * block, block)
            keep[i, :, lanes] = jnp.where(core == 0, low, high)
            send[i, :, lanes] = jnp.where(core == 0, high, low).astype(BF)


def backward(s_all, h_pieces, err, act, slope, w_out, after, n_z, rows, out_rows, slice_w):
    n_t = s_all.shape[0]
    frames, wall = err.shape
    sff, sd = w_out.shape
    wide = out_rows // rows * sd + sff
    return call(
        functools.partial(backward_kernel, (n_t, n_z, rows, out_rows, slice_w)),
        "student_backward",
        [shape((n_z, rows, wide), F32), shape((n_z, rows, wide), BF)],
        [VMEM] + [ANY] * (2 * n_t) + [VMEM] * 4 + [ANY],
        scratch=[
            pltpu.VMEM((sd, wall), BF),
            pltpu.VMEM((sd, frames), BF),
            pltpu.SemaphoreType.DMA((2 * n_t,)),
        ],
        limit=16,
        us=6,
    )(s_all, *h_pieces, err, act, slope, w_out, after)


def add_kernel(own, *refs):
    total = own[...]
    for r in refs[:-1]:
        total = total + r[...].astype(F32)
    refs[-1][...] = total.astype(refs[-1].dtype)


def chip_kernel(n_t, splits, keep, recv, *outs):
    me = lax.axis_index("teacher")
    own, sends = outs[0], outs[1:]
    at = 0
    for first, width in splits:
        w = width // n_t
        for k in range(n_t):
            t = me ^ k if len(sends) > 1 else k
            lanes = pl.ds(pl.multiple_of(first + t * w, 128), w)
            value = keep[:, :, lanes] + recv[:, :, lanes].astype(F32)
            if len(sends) > 1:
                dst = own if k == 0 else sends[k - 1]
                dst[:, :, pl.ds(at, w)] = value.astype(dst.dtype)
            else:
                sends[0][k, :, :, pl.ds(at, w)] = value.astype(BF)

                @pl.when(me == k)
                def _(value=value, at=at, w=w):
                    own[:, :, pl.ds(at, w)] = value

        at += w


def teacher_kernel(n_t, n_z, mine, *refs):
    got, own, sends = refs[: -n_z], refs[-n_z], refs[len(refs) - n_z + 1 :]
    z = lax.axis_index("dp") // 2
    me = lax.axis_index("teacher")
    for k in range(n_z):
        at = z ^ k
        total = mine[at]
        for j in range(1, n_t):
            value = got[0][me ^ j, at] if len(got) == 1 else got[j - 1][at]
            total = total + value.astype(F32)
        dst = own if k == 0 else sends[k - 1]
        dst[...] = total.astype(dst.dtype)


def last_kernel(n_t, *refs):
    heads, rest, (g_in, g_out, g_head) = refs[:n_t], refs[n_t : 2 * n_t], refs[2 * n_t :]
    me = lax.axis_index("teacher")
    rows = g_in.shape[0]
    parts = g_out.shape[0] // rows
    ow, iw, hw = g_out.shape[1] // n_t, g_in.shape[1] // n_t, g_head.shape[1] // n_t
    for k in range(n_t):
        at = me ^ k
        g_head[:, aligned(at, hw, 128)] = heads[k][...]
        for p in range(parts):
            g_out[pl.ds(p * rows, rows), aligned(at, ow, 128)] = rest[k][:, pl.ds(p * ow, ow)]
        g_in[:, aligned(at, iw, 128)] = rest[k][:, pl.ds(parts * ow, iw)]


def make_body(n_t, n_dp):
    n_z = n_dp // 2

    def swap_t(k, value):
        return lax.ppermute(value, "teacher", [(t, t ^ k) for t in range(n_t)])

    def swap_z(k, value):
        return lax.ppermute(value, "dp", [(d, d ^ (2 * k)) for d in range(n_dp)])

    def swap_core(value):
        return lax.ppermute(value, "dp", [(d, d ^ 1) for d in range(n_dp)])

    def body(hid_whisper, hid_beats, hid_wavlm, up_whisper, down_whisper, up_beats, down_beats,
             up_wavlm, down_wavlm, clip_len, send_counts, student_in, w_in, w_out, w_head):
        frames, sd = student_in.shape
        half = frames // 2
        cap = 2 * frames // n_dp
        rows, sff = w_in.shape
        out_rows = w_out.shape[0]
        parts = out_rows // rows
        wall = w_head.shape[1]
        slice_w = wall // n_t
        packed = call(
            functools.partial(pack_kernel, n_t, n_dp, cap), "pack",
            shape((n_dp * rows, (sd + slice_w) // 2), BF), [SMEM, VMEM, VMEM], limit=60,
        )(send_counts, student_in, w_head)
        arrived = lax.all_to_all(packed, "dp", split_axis=0, concat_axis=0, tiled=True)

        merged, hid = call(
            merge_kernel, "merge", [shape((rows, sff + parts * sd), BF), shape((frames, wall), BF)],
            [HBM] * 5 + [ANY], scratch=[pltpu.SemaphoreType.DMA((parts + 4,))], limit=60,
        )(w_in, w_out, hid_whisper, hid_beats, hid_wavlm, packed)
        from_z = [merged] + [swap_z(k, merged) for k in range(1, n_z)]

        from_x, from_y = swap_t(1, hid), swap_t(2, hid)
        to_y, to_x = call(
            halves_kernel, "halves", [shape((half, wall), BF)] * 2, [HBM] * 2,
            scratch=[pltpu.SemaphoreType.DMA((2,))], limit=60,
        )(from_x, from_y)
        group = [hid, from_x, from_y, swap_t(1, to_x), swap_t(2, to_y)]

        s_own, head = call(
            functools.partial(unpack_kernel, n_dp, cap), "unpack",
            [shape((n_t, frames, sd + 128), BF), shape((sd, slice_w // 2), BF)], [SMEM, SMEM, VMEM], limit=60,
        )(send_counts, clip_len, arrived)
        s_all = lax.all_to_all(s_own, "teacher", split_axis=0, concat_axis=0, tiled=True)
        h_mine = [head] + [swap_t(k, head) for k in range(1, n_t)]
        e_parts = ffn(group, (up_whisper, down_whisper, up_beats, down_beats, up_wavlm, down_wavlm), slice_w, s_own)
        from_z, h_mine, _ = lax.optimization_barrier((from_z, h_mine, e_parts[0]))
        w_pieces, h_pieces = [], []
        for piece in from_z:
            w_pieces += [piece, swap_core(piece)]
        for piece in h_mine:
            h_pieces += [piece, swap_core(piece)]

        act, slope, full_out, err, h_keep, h_send = forward(
            s_all, w_pieces, h_pieces[:2], h_mine[1:], e_parts, n_z, rows, out_rows, slice_w, sff
        )
        def chip_sum(keep, send, splits, many):
            chunk = keep.shape[2] // n_t
            sends = [shape((n_z, rows, chunk), BF)] * (n_t - 1) if many else [shape((n_t, n_z, rows, chunk), BF)]
            return call(
                functools.partial(chip_kernel, n_t, splits), "chip",
                [shape((n_z, rows, chunk), F32)] + sends, [VMEM] * 2,
            )(keep, swap_core(send))

        def z_sum(mine, got):
            chunk = mine.shape[2]
            own, *sends = call(
                functools.partial(teacher_kernel, n_t, n_z), "over_teacher",
                [shape((rows, chunk), F32)] + [shape((rows, chunk), BF)] * (n_z - 1), [VMEM] * (1 + len(got)),
            )(mine, *got)
            got = [swap_z(k + 1, v) for k, v in enumerate(sends)]
            total = call(add_kernel, "over_z", shape((rows, chunk), F32), [VMEM] * n_z)(own, *got)
            return [total] + [swap_t(k, total) for k in range(1, n_t)]

        h_own, h_out = chip_sum(h_keep, h_send, [(0, wall)], False)
        h_got = lax.all_to_all(h_out, "teacher", split_axis=0, concat_axis=0, tiled=True)
        keep, send = backward(s_all, h_pieces, err, act, slope, full_out, h_own, n_z, rows, out_rows, slice_w)
        splits = [(p * sd, sd) for p in range(parts)] + [(parts * sd, sff)]
        r_own, *r_sends = chip_sum(keep, send, splits, True)
        r_got = [swap_t(k + 1, v) for k, v in enumerate(r_sends)]
        h_all = z_sum(h_own, [h_got])
        r_all = z_sum(r_own, r_got)
        grad_in, grad_out, grad_head = call(
            functools.partial(last_kernel, n_t), "last",
            [shape((rows, sff), F32), shape((out_rows, sd), F32), shape((rows, wall), F32)], [VMEM] * (2 * n_t),
        )(*h_all, *r_all)
        return grad_in, grad_out, grad_head

    return body


def solution(mesh):
    rows = P(("teacher", "dp"), None)
    in_specs = (
        rows, rows, rows,
        P(None, "teacher"), P("teacher", None),
        P(None, "teacher"), P("teacher", None),
        P(None, "teacher"), P("teacher", None),
        P(("teacher", "dp")), P("teacher", None, None), rows,
        P("dp", None), P("dp", None), P("dp", None),
    )
    out_specs = (P("dp", None), P("dp", None), P("dp", None))
    body = make_body(mesh.shape["teacher"], mesh.shape["dp"])
    return jax.shard_map(body, mesh=mesh, in_specs=in_specs, out_specs=out_specs, check_vma=False)
```

profile of v0, /device:TPU:0, one launch (start us, length us, event | category | flops | bytes accessed | tf_op | source)
XLA Modules:
  0.0 169.9 jit_solution(10953310811332173518)
XLA Ops:
  0.6 2.2 %pack.1.after = bf16[512,640]{1,0:T(8,128)(2,1)} custom-call(s32[1,8,8]{2,1,0:T(8,128)} %table.3, bf16[128,512]{1,0:T(8,128)(2,1)} %student.1, bf16[64,3072]{1,0:T(8,128)(2,1)} %w_head.1), custom_call_target="tpu_custom_call" | custom-call | flops 1000000000 | bytes 3000000 | tf_op jit(solution)/shard_map/pack/pallas_call | solution.py:426
  2.9 2.4 %merge.1 = (bf16[64,3072]{1,0:T(8,128)(2,1)}, bf16[128,3072]{1,0:T(8,128)(2,1)}) custom-call(bf16[64,1536]{1,0:T(8,128)(2,1)} %w_in.1, bf16[192,512]{1,0:T(8,128)(2,1)} %w_out.1, bf16[128,1280]{1,0:T(8,128)(2,1)} %whisper.1, bf16[128,768]{1,0:T(8,128)(2,1)} %beats.1, bf16[128,1024]{1,0:T(8,128)(2,1)} %wavlm.1, bf16[512,640]{1,0:T(8,128)(2,1)} %pack.1.after), custom_call_target="tpu_custom_call" | custom-call | flops 1000000000 | bytes 3000000 | tf_op jit(solution)/shard_map/merge/pallas_call | solution.py:432
  5.2 3.0 %collective-permute-start.6 = (bf16[128,3072]{1,0:T(8,128)(2,1)}, bf16[128,3072]{1,0:T(8,128)(2,1)S(1)}, u32[]{:S(2)}, u32[]{:S(2)}) collective-permute-start(bf16[128,3072]{1,0:T(8,128)(2,1)} %get-tuple-element.45.refs_0_), channel_id=1, source_target_pairs={{0,8},{8,0},{16,24},{24,16},{1,9},{9,1},{17,25},{25,17},{2,10},{10... | collective-permute-start | bytes 2359304 | tf_op jit(solution)/shard_map/ppermute | solution.py:408
  9.8 4.9 %all-to-all-start = ((bf16[8,64,640]{2,1,0:T(8,128)(2,1)}), bf16[8,64,640]{2,1,0:T(8,128)(2,1)S(1)}, u32[]{:S(2)}, u32[]{:S(2)}) async-start(bf16[8,64,640]{2,1,0:T(8,128)(2,1)} %bitcast), calls=%async_computation | async-start | bytes 1310720 | tf_op jit(solution)/shard_map/all_to_all | solution.py:430
  14.6 2.0 %collective-permute-start = (bf16[64,3072]{1,0:T(8,128)(2,1)}, bf16[64,3072]{1,0:T(8,128)(2,1)}, u32[]{:S(2)}, u32[]{:S(2)}) collective-permute-start(bf16[64,3072]{1,0:T(8,128)(2,1)} %get-tuple-element.49.refs_1_), channel_id=1, source_target_pairs={{0,2},{1,3},{2,0},{3,1},{4,6},{5,7},{6,4},{7,5},{8,10},{9,11},{10,... | collective-permute-start | bytes 1179656 | tf_op jit(solution)/shard_map/ppermute | solution.py:411
  16.7 9.3 %collective-permute-done.6.from_x.refs_1_ = bf16[128,3072]{1,0:T(8,128)(2,1)S(1)} collective-permute-done((bf16[128,3072]{1,0:T(8,128)(2,1)}, bf16[128,3072]{1,0:T(8,128)(2,1)S(1)}, u32[]{:S(2)}, u32[]{:S(2)}) %collective-permute-start.6) | collective-permute-done | bytes 786464 | tf_op jit(solution)/shard_map/ppermute | solution.py:408
  28.4 2.0 %halves.1 = (bf16[64,3072]{1,0:T(8,128)(2,1)}, bf16[64,3072]{1,0:T(8,128)(2,1)}) custom-call(bf16[128,3072]{1,0:T(8,128)(2,1)} %copy-done.5, bf16[128,3072]{1,0:T(8,128)(2,1)} %copy-done.7), custom_call_target="tpu_custom_call" | custom-call | flops 1000000000 | bytes 3000000 | tf_op jit(solution)/shard_map/halves/pallas_call | solution.py:439
  33.2 2.6 %collective-permute-start.1 = (bf16[64,3072]{1,0:T(8,128)(2,1)S(1)}, bf16[64,3072]{1,0:T(8,128)(2,1)}, u32[]{:S(2)}, u32[]{:S(2)}) collective-permute-start(bf16[64,3072]{1,0:T(8,128)(2,1)S(1)} %copy-done.13), channel_id=1, source_target_pairs={{0,4},{1,5},{2,6},{3,7},{4,0},{5,1},{6,2},{7,3},{8,12},{9,13},{10,... | collective-permute-start | bytes 1179656 | tf_op jit(solution)/shard_map/ppermute | solution.py:411
  38.6 2.4 %unpack.1 = (bf16[4,128,640]{2,1,0:T(8,128)(2,1)}, bf16[512,384]{1,0:T(8,128)(2,1)}) custom-call(s32[1,8,8]{2,1,0:T(8,128)} %table.3, s32[1]{0:T(128)S(6)} %copy.18.clip_len, bf16[512,640]{1,0:T(8,128)(2,1)} %bitcast.2), custom_call_target="tpu_custom_call" | custom-call | flops 1000000000 | bytes 3000000 | tf_op jit(solution)/shard_map/unpack/pallas_call | solution.py:445
  41.0 3.5 %all-to-all-start.1 = ((bf16[4,128,640]{2,1,0:T(8,128)(2,1)}), bf16[4,128,640]{2,1,0:T(8,128)(2,1)S(1)}, u32[]{:S(2)}, u32[]{:S(2)}) async-start(bf16[4,128,640]{2,1,0:T(8,128)(2,1)} %get-tuple-element.42.refs_11_), calls=%async_computation.1 | async-start | bytes 1310720 | tf_op jit(solution)/shard_map/all_to_all | solution.py:449
  44.5 2.0 %collective-permute-start.3 = (bf16[512,384]{1,0:T(8,128)(2,1)}, bf16[512,384]{1,0:T(8,128)(2,1)S(1)}, u32[]{:S(2)}, u32[]{:S(2)}) collective-permute-start(bf16[512,384]{1,0:T(8,128)(2,1)} %get-tuple-element.53.refs_9_.refs_1_), channel_id=1, source_target_pairs={{0,8},{8,0},{16,24},{24,16},{1,9},{9,1},{17,25},{25,17},{2,10},{10... | collective-permute-start | bytes 1179656 | tf_op jit(solution)/shard_map/ppermute | solution.py:408
  49.2 14.3 %ffn.1 = (f32[512,1280]{1,0:T(8,128)}, f32[512,768]{1,0:T(8,128)}, f32[512,1024]{1,0:T(8,128)}) custom-call(bf16[128,3072]{1,0:T(8,128)(2,1)S(1)} %copy-done.4, bf16[128,3072]{1,0:T(8,128)(2,1)S(1)} %copy-done.6, bf16[128,3072]{1,0:T(8,128)(2,1)S(1)} %copy-done.8, bf16[64,3072]{1,0:T(8,128)(2,1)} %collective-permute-done.8.refs_3_, ...), custom_call_target="tpu_custom_call" | custom-call | flops 12999999488 | bytes 39000000 | tf_op jit(solution)/shard_map/ffn/pallas_call | solution.py:185
  65.3 4.7 %collective-permute-done.5.refs_13_.refs_7_ = bf16[512,384]{1,0:T(8,128)(2,1)S(1)} collective-permute-done((bf16[512,384]{1,0:T(8,128)(2,1)}, bf16[512,384]{1,0:T(8,128)(2,1)S(1)}, u32[]{:S(2)}, u32[]{:S(2)}) %collective-permute-start.5) | collective-permute-done | bytes 393248 | tf_op jit(solution)/shard_map/ppermute | solution.py:408
  77.9 1.7 %copy-done.23 = f32[512,1280]{1,0:T(8,128)S(1)} copy-done((f32[512,1280]{1,0:T(8,128)S(1)}, f32[512,1280]{1,0:T(8,128)}, u32[]{:S(2)}) %copy-start.23) | copy-done | bytes 2621464
  79.7 1.6 copy-done.24
  82.7 7.4 %student_forward.1 = (bf16[512,1536]{1,0:T(8,128)(2,1)S(1)}, f32[512,1536]{1,0:T(8,128)S(1)}, bf16[1536,512]{1,0:T(8,128)(2,1)S(1)}, bf16[512,3072]{1,0:T(8,128)...) custom-call(bf16[4,128,640]{2,1,0:T(8,128)(2,1)S(1)} %all-to-all-done.1.refs_0_, ...), custom_call_target="tpu_custom_call" | custom-call | flops 7000000000 | bytes 21000000 | tf_op jit(solution)/shard_map/student_forward/pallas_call | solution.py:259
  91.2 2.4 %collective-permute-done.15.recv = bf16[4,64,3072]{2,1,0:T(8,128)(2,1)S(1)} collective-permute-done((bf16[4,64,3072]{2,1,0:T(8,128)(2,1)S(1)}, bf16[4,64,3072]{2,1,0:T(8,128)(2,1)S(1)}, u32[]{:S(2)}, u32[]{:S(2)}) %collective-permute-start.15) | collective-permute-done | bytes 1572896 | tf_op jit(solution)/shard_map/ppermute | solution.py:414
  95.3 7.6 %student_backward.1 = (f32[4,64,3072]{2,1,0:T(8,128)S(1)}, bf16[4,64,3072]{2,1,0:T(8,128)(2,1)}) custom-call(bf16[4,128,640]{2,1,0:T(8,128)(2,1)S(1)} %copy-done.2, bf16[512,384]{1,0:T(8,128)(2,1)} %get-tuple-element.53.refs_9_.refs_1_, bf16[512,384]{1,0:T(8,128)(2,1)S(1)} %copy-done.22, bf16[512,384]{1,0:T(8,128)(2,1)S(1)} %copy-done.15, ...), custom_call_target="tpu_custom_call" | custom-call | flops 6000000000 | bytes 18000000 | tf_op jit(solution)/shard_map/student_backward/pallas_call | solution.py:331
  103.1 4.6 %all-to-all-start.2 = ((bf16[4,4,64,768]{3,2,1,0:T(8,128)(2,1)}), bf16[4,4,64,768]{3,2,1,0:T(8,128)(2,1)}, u32[]{:S(2)}, u32[]{:S(2)}) async-start(bf16[4,4,64,768]{3,2,1,0:T(8,128)(2,1)} %copy-done), calls=%async_computation.2 | async-start | bytes 3145728 | tf_op jit(solution)/shard_map/all_to_all | solution.py:481
  107.7 2.9 %chip.3 = (f32[4,64,768]{2,1,0:T(8,128)S(1)}, bf16[4,64,768]{2,1,0:T(8,128)(2,1)}, bf16[4,64,768]{2,1,0:T(8,128)(2,1)}, bf16[4,64,768]{2,1,0:T(8,128)(2,1)S(1)}) custom-call(f32[4,64,3072]{2,1,0:T(8,128)S(1)} %get-tuple-element.71.keep, bf16[4,64,3072]{2,1,0:T(8,128)(2,1)} %collective-permute-done.25.recv), custom_call_target="tpu_custom_call" | custom-call | flops 1000000000 | bytes 3000000 | tf_op jit(solution)/shard_map/chip/pallas_call | solution.py:465
  111.4 1.8 %collective-permute-start.26 = (bf16[4,64,768]{2,1,0:T(8,128)(2,1)}, bf16[4,64,768]{2,1,0:T(8,128)(2,1)S(1)}, u32[]{:S(2)}, u32[]{:S(2)}) collective-permute-start(bf16[4,64,768]{2,1,0:T(8,128)(2,1)} %get-tuple-element.74), channel_id=1, source_target_pairs={{0,8},{8,0},{16,24},{24,16},{1,9},{9,1},{17,25},{25,17},{2,10},{10... | collective-permute-start | bytes 1179656 | tf_op jit(solution)/shard_map/ppermute | solution.py:408
  114.9 13.2 %all-to-all-done.2.refs_0_ = bf16[4,4,64,768]{3,2,1,0:T(8,128)(2,1)} async-done(((bf16[4,4,64,768]{3,2,1,0:T(8,128)(2,1)}), bf16[4,4,64,768]{3,2,1,0:T(8,128)(2,1)}, u32[]{:S(2)}, u32[]{:S(2)}) %all-to-all-start.2) | async-done | bytes 1572896 | tf_op jit(solution)/shard_map/all_to_all | solution.py:481
  132.1 2.1 %collective-permute-start.17 = (bf16[64,768]{1,0:T(8,128)(2,1)S(1)}, bf16[64,768]{1,0:T(8,128)(2,1)S(1)}, u32[]{:S(2)}, u32[]{:S(2)}) collective-permute-start(bf16[64,768]{1,0:T(8,128)(2,1)S(1)} %get-tuple-element.65), channel_id=1, source_target_pairs={{0,4},{1,5},{2,6},{3,7},{4,0},{5,1},{6,2},{7,3},{8,12},{9,13},{10,... | collective-permute-start | bytes 294920 | tf_op jit(solution)/shard_map/ppermute | solution.py:411
  134.2 2.2 %collective-permute-done.16.refs_0_ = bf16[64,768]{1,0:T(8,128)(2,1)S(1)} collective-permute-done((bf16[64,768]{1,0:T(8,128)(2,1)S(1)}, bf16[64,768]{1,0:T(8,128)(2,1)S(1)}, u32[]{:S(2)}, u32[]{:S(2)}) %collective-permute-start.16) | collective-permute-done | bytes 98336 | tf_op jit(solution)/shard_map/ppermute | solution.py:411
  136.4 2.1 %collective-permute-start.18 = (bf16[64,768]{1,0:T(8,128)(2,1)S(1)}, bf16[64,768]{1,0:T(8,128)(2,1)S(1)}, u32[]{:S(2)}, u32[]{:S(2)}) collective-permute-start(bf16[64,768]{1,0:T(8,128)(2,1)S(1)} %get-tuple-element.66), channel_id=1, source_target_pairs={{0,6},{1,7},{2,4},{3,5},{4,2},{5,3},{6,0},{7,1},{8,14},{9,15},{10,... | collective-permute-start | bytes 294920 | tf_op jit(solution)/shard_map/ppermute | solution.py:411
  138.5 2.4 %collective-permute-done.17.refs_1_ = bf16[64,768]{1,0:T(8,128)(2,1)S(1)} collective-permute-done((bf16[64,768]{1,0:T(8,128)(2,1)S(1)}, bf16[64,768]{1,0:T(8,128)(2,1)S(1)}, u32[]{:S(2)}, u32[]{:S(2)}) %collective-permute-start.17) | collective-permute-done | bytes 98336 | tf_op jit(solution)/shard_map/ppermute | solution.py:411
  141.0 2.0 %collective-permute-done.18.refs_2_ = bf16[64,768]{1,0:T(8,128)(2,1)S(1)} collective-permute-done((bf16[64,768]{1,0:T(8,128)(2,1)S(1)}, bf16[64,768]{1,0:T(8,128)(2,1)S(1)}, u32[]{:S(2)}, u32[]{:S(2)}) %collective-permute-start.18) | collective-permute-done | bytes 98336 | tf_op jit(solution)/shard_map/ppermute | solution.py:411
  146.7 2.5 %collective-permute-start.30 = (bf16[64,768]{1,0:T(8,128)(2,1)S(1)}, bf16[64,768]{1,0:T(8,128)(2,1)S(1)}, u32[]{:S(2)}, u32[]{:S(2)}) collective-permute-start(bf16[64,768]{1,0:T(8,128)(2,1)S(1)} %get-tuple-element.79), channel_id=1, source_target_pairs={{0,4},{1,5},{2,6},{3,7},{4,0},{5,1},{6,2},{7,3},{8,12},{9,13},{10,... | collective-permute-start | bytes 294920 | tf_op jit(solution)/shard_map/ppermute | solution.py:411
  152.5 4.7 %collective-permute-done.30.refs_1_ = bf16[64,768]{1,0:T(8,128)(2,1)S(1)} collective-permute-done((bf16[64,768]{1,0:T(8,128)(2,1)S(1)}, bf16[64,768]{1,0:T(8,128)(2,1)S(1)}, u32[]{:S(2)}, u32[]{:S(2)}) %collective-permute-start.30) | collective-permute-done | bytes 98336 | tf_op jit(solution)/shard_map/ppermute | solution.py:411
  158.6 2.1 %collective-permute-start.34 = (f32[64,768]{1,0:T(8,128)S(1)}, f32[64,768]{1,0:T(8,128)S(1)}, u32[]{:S(2)}, u32[]{:S(2)}) collective-permute-start(f32[64,768]{1,0:T(8,128)S(1)} %over_z.3.refs_4_), channel_id=1, source_target_pairs={{0,24},{8,16},{16,8},{24,0},{1,25},{9,17},{17,9},{25,1},{2,26},{10... | collective-permute-start | bytes 589832 | tf_op jit(solution)/shard_map/ppermute | solution.py:408
  160.7 2.1 %collective-permute-done.20.refs_2_ = f32[64,768]{1,0:T(8,128)S(1)} collective-permute-done((f32[64,768]{1,0:T(8,128)S(1)}, f32[64,768]{1,0:T(8,128)S(1)}, u32[]{:S(2)}, u32[]{:S(2)}) %collective-permute-start.20) | collective-permute-done | bytes 196640 | tf_op jit(solution)/shard_map/ppermute | solution.py:408
  164.0 4.5 %collective-permute-done.33.refs_6_ = f32[64,768]{1,0:T(8,128)S(1)} collective-permute-done((f32[64,768]{1,0:T(8,128)S(1)}, f32[64,768]{1,0:T(8,128)S(1)}, u32[]{:S(2)}, u32[]{:S(2)}) %collective-permute-start.33) | collective-permute-done | bytes 196640 | tf_op jit(solution)/shard_map/ppermute | solution.py:408
  (112 shorter events, 43.1 us)
Async XLA Ops:
  5.2 20.8 %collective-permute-start.6 = (bf16[128,3072]{1,0:T(8,128)(2,1)}, bf16[128,3072]{1,0:T(8,128)(2,1)S(1)}, u32[]{:S(2)}, u32[]{:S(2)}) collective-permute-start(bf16[128,3072]{1,0:T(8,128)(2,1)} %get-tuple-element.45.refs_0_), channel_id=1, source_target_pairs={{0,8},{8,0},{16,24},{24,16},{1,9},{9,1},{17,25},{25,17},{2,10},{10... | collective-permute-start | bytes 2359304 | tf_op jit(solution)/shard_map/ppermute | solution.py:408
  8.2 19.2 %collective-permute-start.7 = (bf16[128,3072]{1,0:T(8,128)(2,1)}, bf16[128,3072]{1,0:T(8,128)(2,1)S(1)}, u32[]{:S(2)}, u32[]{:S(2)}) collective-permute-start(bf16[128,3072]{1,0:T(8,128)(2,1)} %get-tuple-element.45.refs_0_), channel_id=1, source_target_pairs={{0,16},{8,24},{16,0},{24,8},{1,17},{9,25},{17,1},{25,9},{2,18},{10... | collective-permute-start | bytes 2359304 | tf_op jit(solution)/shard_map/ppermute | solution.py:408
  9.8 28.0 %all-to-all-start = ((bf16[8,64,640]{2,1,0:T(8,128)(2,1)}), bf16[8,64,640]{2,1,0:T(8,128)(2,1)S(1)}, u32[]{:S(2)}, u32[]{:S(2)}) async-start(bf16[8,64,640]{2,1,0:T(8,128)(2,1)} %bitcast), calls=%async_computation | async-start | bytes 1310720 | tf_op jit(solution)/shard_map/all_to_all | solution.py:430
  14.6 29.9 %collective-permute-start = (bf16[64,3072]{1,0:T(8,128)(2,1)}, bf16[64,3072]{1,0:T(8,128)(2,1)}, u32[]{:S(2)}, u32[]{:S(2)}) collective-permute-start(bf16[64,3072]{1,0:T(8,128)(2,1)} %get-tuple-element.49.refs_1_), channel_id=1, source_target_pairs={{0,2},{1,3},{2,0},{3,1},{4,6},{5,7},{6,4},{7,5},{8,10},{9,11},{10,... | collective-permute-start | bytes 1179656 | tf_op jit(solution)/shard_map/ppermute | solution.py:411
  30.4 16.1 %collective-permute-start.8 = (bf16[64,3072]{1,0:T(8,128)(2,1)}, bf16[64,3072]{1,0:T(8,128)(2,1)}, u32[]{:S(2)}, u32[]{:S(2)}) collective-permute-start(bf16[64,3072]{1,0:T(8,128)(2,1)} %get-tuple-element.46), channel_id=1, source_target_pairs={{0,8},{8,0},{16,24},{24,16},{1,9},{9,1},{17,25},{25,17},{2,10},{10... | collective-permute-start | bytes 1179656 | tf_op jit(solution)/shard_map/ppermute | solution.py:408
  31.7 16.3 %collective-permute-start.9 = (bf16[64,3072]{1,0:T(8,128)(2,1)}, bf16[64,3072]{1,0:T(8,128)(2,1)}, u32[]{:S(2)}, u32[]{:S(2)}) collective-permute-start(bf16[64,3072]{1,0:T(8,128)(2,1)} %get-tuple-element.47), channel_id=1, source_target_pairs={{0,16},{8,24},{16,0},{24,8},{1,17},{9,25},{17,1},{25,9},{2,18},{10... | collective-permute-start | bytes 1179656 | tf_op jit(solution)/shard_map/ppermute | solution.py:408
  33.2 30.3 %collective-permute-start.1 = (bf16[64,3072]{1,0:T(8,128)(2,1)S(1)}, bf16[64,3072]{1,0:T(8,128)(2,1)}, u32[]{:S(2)}, u32[]{:S(2)}) collective-permute-start(bf16[64,3072]{1,0:T(8,128)(2,1)S(1)} %copy-done.13), channel_id=1, source_target_pairs={{0,4},{1,5},{2,6},{3,7},{4,0},{5,1},{6,2},{7,3},{8,12},{9,13},{10,... | collective-permute-start | bytes 1179656 | tf_op jit(solution)/shard_map/ppermute | solution.py:411
  35.8 27.8 %collective-permute-start.2 = (bf16[64,3072]{1,0:T(8,128)(2,1)S(1)}, bf16[64,3072]{1,0:T(8,128)(2,1)}, u32[]{:S(2)}, u32[]{:S(2)}) collective-permute-start(bf16[64,3072]{1,0:T(8,128)(2,1)S(1)} %copy-done.13), channel_id=1, source_target_pairs={{0,6},{1,7},{2,4},{3,5},{4,2},{5,3},{6,0},{7,1},{8,14},{9,15},{10,... | collective-permute-start | bytes 1179656 | tf_op jit(solution)/shard_map/ppermute | solution.py:411
  41.0 30.7 %all-to-all-start.1 = ((bf16[4,128,640]{2,1,0:T(8,128)(2,1)}), bf16[4,128,640]{2,1,0:T(8,128)(2,1)S(1)}, u32[]{:S(2)}, u32[]{:S(2)}) async-start(bf16[4,128,640]{2,1,0:T(8,128)(2,1)} %get-tuple-element.42.refs_11_), calls=%async_computation.1 | async-start | bytes 1310720 | tf_op jit(solution)/shard_map/all_to_all | solution.py:449
  44.5 19.2 %collective-permute-start.3 = (bf16[512,384]{1,0:T(8,128)(2,1)}, bf16[512,384]{1,0:T(8,128)(2,1)S(1)}, u32[]{:S(2)}, u32[]{:S(2)}) collective-permute-start(bf16[512,384]{1,0:T(8,128)(2,1)} %get-tuple-element.53.refs_9_.refs_1_), channel_id=1, source_target_pairs={{0,8},{8,0},{16,24},{24,16},{1,9},{9,1},{17,25},{25,17},{2,10},{10... | collective-permute-start | bytes 1179656 | tf_op jit(solution)/shard_map/ppermute | solution.py:408
  46.5 18.0 %collective-permute-start.4 = (bf16[512,384]{1,0:T(8,128)(2,1)}, bf16[512,384]{1,0:T(8,128)(2,1)S(1)}, u32[]{:S(2)}, u32[]{:S(2)}) collective-permute-start(bf16[512,384]{1,0:T(8,128)(2,1)} %get-tuple-element.53.refs_9_.refs_1_), channel_id=1, source_target_pairs={{0,16},{8,24},{16,0},{24,8},{1,17},{9,25},{17,1},{25,9},{2,18},{10... | collective-permute-start | bytes 1179656 | tf_op jit(solution)/shard_map/ppermute | solution.py:408
  48.0 22.0 %collective-permute-start.5 = (bf16[512,384]{1,0:T(8,128)(2,1)}, bf16[512,384]{1,0:T(8,128)(2,1)S(1)}, u32[]{:S(2)}, u32[]{:S(2)}) collective-permute-start(bf16[512,384]{1,0:T(8,128)(2,1)} %get-tuple-element.53.refs_9_.refs_1_), channel_id=1, source_target_pairs={{0,24},{8,16},{16,8},{24,0},{1,25},{9,17},{17,9},{25,1},{2,26},{10... | collective-permute-start | bytes 1179656 | tf_op jit(solution)/shard_map/ppermute | solution.py:408
  90.3 4.8 %collective-permute-start.22 = (bf16[512,384]{1,0:T(8,128)(2,1)S(1)}, bf16[512,384]{1,0:T(8,128)(2,1)S(1)}, u32[]{:S(2)}, u32[]{:S(2)}) collective-permute-start(bf16[512,384]{1,0:T(8,128)(2,1)S(1)} %copy-done.15), channel_id=1, source_target_pairs={{0,1},{1,0},{2,3},{3,2},{4,5},{5,4},{6,7},{7,6},{8,9},{9,8},{10,11... | collective-permute-start | bytes 1179656 | tf_op jit(solution)/shard_map/ppermute | solution.py:414
  90.7 4.4 %collective-permute-start.23 = (bf16[512,384]{1,0:T(8,128)(2,1)S(1)}, bf16[512,384]{1,0:T(8,128)(2,1)S(1)}, u32[]{:S(2)}, u32[]{:S(2)}) collective-permute-start(bf16[512,384]{1,0:T(8,128)(2,1)S(1)} %copy-done.17), channel_id=1, source_target_pairs={{0,1},{1,0},{2,3},{3,2},{4,5},{5,4},{6,7},{7,6},{8,9},{9,8},{10,11... | collective-permute-start | bytes 1179656 | tf_op jit(solution)/shard_map/ppermute | solution.py:414
  90.9 4.5 %collective-permute-start.24 = (bf16[512,384]{1,0:T(8,128)(2,1)S(1)}, bf16[512,384]{1,0:T(8,128)(2,1)S(1)}, u32[]{:S(2)}, u32[]{:S(2)}) collective-permute-start(bf16[512,384]{1,0:T(8,128)(2,1)S(1)} %copy-done.19), channel_id=1, source_target_pairs={{0,1},{1,0},{2,3},{3,2},{4,5},{5,4},{6,7},{7,6},{8,9},{9,8},{10,11... | collective-permute-start | bytes 1179656 | tf_op jit(solution)/shard_map/ppermute | solution.py:414
  102.9 4.8 %collective-permute-start.25 = (bf16[4,64,3072]{2,1,0:T(8,128)(2,1)}, bf16[4,64,3072]{2,1,0:T(8,128)(2,1)}, u32[]{:S(2)}, u32[]{:S(2)}) collective-permute-start(bf16[4,64,3072]{2,1,0:T(8,128)(2,1)} %get-tuple-element.72), channel_id=1, source_target_pairs={{0,1},{1,0},{2,3},{3,2},{4,5},{5,4},{6,7},{7,6},{8,9},{9,8},{10,11... | collective-permute-start | bytes 4718600 | tf_op jit(solution)/shard_map/ppermute | solution.py:414
  103.1 25.0 %all-to-all-start.2 = ((bf16[4,4,64,768]{3,2,1,0:T(8,128)(2,1)}), bf16[4,4,64,768]{3,2,1,0:T(8,128)(2,1)}, u32[]{:S(2)}, u32[]{:S(2)}) async-start(bf16[4,4,64,768]{3,2,1,0:T(8,128)(2,1)} %copy-done), calls=%async_computation.2 | async-start | bytes 3145728 | tf_op jit(solution)/shard_map/all_to_all | solution.py:481
  111.4 33.1 %collective-permute-start.26 = (bf16[4,64,768]{2,1,0:T(8,128)(2,1)}, bf16[4,64,768]{2,1,0:T(8,128)(2,1)S(1)}, u32[]{:S(2)}, u32[]{:S(2)}) collective-permute-start(bf16[4,64,768]{2,1,0:T(8,128)(2,1)} %get-tuple-element.74), channel_id=1, source_target_pairs={{0,8},{8,0},{16,24},{24,16},{1,9},{9,1},{17,25},{25,17},{2,10},{10... | collective-permute-start | bytes 1179656 | tf_op jit(solution)/shard_map/ppermute | solution.py:408
  113.2 31.3 %collective-permute-start.27 = (bf16[4,64,768]{2,1,0:T(8,128)(2,1)}, bf16[4,64,768]{2,1,0:T(8,128)(2,1)S(1)}, u32[]{:S(2)}, u32[]{:S(2)}) collective-permute-start(bf16[4,64,768]{2,1,0:T(8,128)(2,1)} %get-tuple-element.75), channel_id=1, source_target_pairs={{0,16},{8,24},{16,0},{24,8},{1,17},{9,25},{17,1},{25,9},{2,18},{10... | collective-permute-start | bytes 1179656 | tf_op jit(solution)/shard_map/ppermute | solution.py:408
  114.7 31.1 %collective-permute-start.28 = (bf16[4,64,768]{2,1,0:T(8,128)(2,1)S(1)}, bf16[4,64,768]{2,1,0:T(8,128)(2,1)S(1)}, u32[]{:S(2)}, u32[]{:S(2)}) collective-permute-start(bf16[4,64,768]{2,1,0:T(8,128)(2,1)S(1)} %get-tuple-element.76), channel_id=1, source_target_pairs={{0,24},{8,16},{16,8},{24,0},{1,25},{9,17},{17,9},{25,1},{2,26},{10... | collective-permute-start | bytes 1179656 | tf_op jit(solution)/shard_map/ppermute | solution.py:408
  130.9 5.6 %collective-permute-start.16 = (bf16[64,768]{1,0:T(8,128)(2,1)S(1)}, bf16[64,768]{1,0:T(8,128)(2,1)S(1)}, u32[]{:S(2)}, u32[]{:S(2)}) collective-permute-start(bf16[64,768]{1,0:T(8,128)(2,1)S(1)} %get-tuple-element.64), channel_id=1, source_target_pairs={{0,2},{1,3},{2,0},{3,1},{4,6},{5,7},{6,4},{7,5},{8,10},{9,11},{10,... | collective-permute-start | bytes 294920 | tf_op jit(solution)/shard_map/ppermute | solution.py:411
  132.1 8.9 %collective-permute-start.17 = (bf16[64,768]{1,0:T(8,128)(2,1)S(1)}, bf16[64,768]{1,0:T(8,128)(2,1)S(1)}, u32[]{:S(2)}, u32[]{:S(2)}) collective-permute-start(bf16[64,768]{1,0:T(8,128)(2,1)S(1)} %get-tuple-element.65), channel_id=1, source_target_pairs={{0,4},{1,5},{2,6},{3,7},{4,0},{5,1},{6,2},{7,3},{8,12},{9,13},{10,... | collective-permute-start | bytes 294920 | tf_op jit(solution)/shard_map/ppermute | solution.py:411
  136.4 6.5 %collective-permute-start.18 = (bf16[64,768]{1,0:T(8,128)(2,1)S(1)}, bf16[64,768]{1,0:T(8,128)(2,1)S(1)}, u32[]{:S(2)}, u32[]{:S(2)}) collective-permute-start(bf16[64,768]{1,0:T(8,128)(2,1)S(1)} %get-tuple-element.66), channel_id=1, source_target_pairs={{0,6},{1,7},{2,4},{3,5},{4,2},{5,3},{6,0},{7,1},{8,14},{9,15},{10,... | collective-permute-start | bytes 294920 | tf_op jit(solution)/shard_map/ppermute | solution.py:411
  143.0 15.7 %collective-permute-start.19 = (f32[64,768]{1,0:T(8,128)S(1)}, f32[64,768]{1,0:T(8,128)S(1)}, u32[]{:S(2)}, u32[]{:S(2)}) collective-permute-start(f32[64,768]{1,0:T(8,128)S(1)} %over_z.2.refs_0_), channel_id=1, source_target_pairs={{0,8},{8,0},{16,24},{24,16},{1,9},{9,1},{17,25},{25,17},{2,10},{10... | collective-permute-start | bytes 589832 | tf_op jit(solution)/shard_map/ppermute | solution.py:408
  146.0 5.9 %collective-permute-start.29 = (bf16[64,768]{1,0:T(8,128)(2,1)S(1)}, bf16[64,768]{1,0:T(8,128)(2,1)S(1)}, u32[]{:S(2)}, u32[]{:S(2)}) collective-permute-start(bf16[64,768]{1,0:T(8,128)(2,1)S(1)} %get-tuple-element.78), channel_id=1, source_target_pairs={{0,2},{1,3},{2,0},{3,1},{4,6},{5,7},{6,4},{7,5},{8,10},{9,11},{10,... | collective-permute-start | bytes 294920 | tf_op jit(solution)/shard_map/ppermute | solution.py:411
  146.7 10.5 %collective-permute-start.30 = (bf16[64,768]{1,0:T(8,128)(2,1)S(1)}, bf16[64,768]{1,0:T(8,128)(2,1)S(1)}, u32[]{:S(2)}, u32[]{:S(2)}) collective-permute-start(bf16[64,768]{1,0:T(8,128)(2,1)S(1)} %get-tuple-element.79), channel_id=1, source_target_pairs={{0,4},{1,5},{2,6},{3,7},{4,0},{5,1},{6,2},{7,3},{8,12},{9,13},{10,... | collective-permute-start | bytes 294920 | tf_op jit(solution)/shard_map/ppermute | solution.py:411
  149.2 8.0 %collective-permute-start.31 = (bf16[64,768]{1,0:T(8,128)(2,1)S(1)}, bf16[64,768]{1,0:T(8,128)(2,1)S(1)}, u32[]{:S(2)}, u32[]{:S(2)}) collective-permute-start(bf16[64,768]{1,0:T(8,128)(2,1)S(1)} %get-tuple-element.80), channel_id=1, source_target_pairs={{0,6},{1,7},{2,4},{3,5},{4,2},{5,3},{6,0},{7,1},{8,14},{9,15},{10,... | collective-permute-start | bytes 294920 | tf_op jit(solution)/shard_map/ppermute | solution.py:411
  150.5 12.3 %collective-permute-start.20 = (f32[64,768]{1,0:T(8,128)S(1)}, f32[64,768]{1,0:T(8,128)S(1)}, u32[]{:S(2)}, u32[]{:S(2)}) collective-permute-start(f32[64,768]{1,0:T(8,128)S(1)} %over_z.2.refs_0_), channel_id=1, source_target_pairs={{0,16},{8,24},{16,0},{24,8},{1,17},{9,25},{17,1},{25,9},{2,18},{10... | collective-permute-start | bytes 589832 | tf_op jit(solution)/shard_map/ppermute | solution.py:408
  151.8 11.0 %collective-permute-start.21 = (f32[64,768]{1,0:T(8,128)S(1)}, f32[64,768]{1,0:T(8,128)S(1)}, u32[]{:S(2)}, u32[]{:S(2)}) collective-permute-start(f32[64,768]{1,0:T(8,128)S(1)} %over_z.2.refs_0_), channel_id=1, source_target_pairs={{0,24},{8,16},{16,8},{24,0},{1,25},{9,17},{17,9},{25,1},{2,26},{10... | collective-permute-start | bytes 589832 | tf_op jit(solution)/shard_map/ppermute | solution.py:408
  157.2 6.9 %collective-permute-start.32 = (f32[64,768]{1,0:T(8,128)S(1)}, f32[64,768]{1,0:T(8,128)S(1)}, u32[]{:S(2)}, u32[]{:S(2)}) collective-permute-start(f32[64,768]{1,0:T(8,128)S(1)} %over_z.3.refs_4_), channel_id=1, source_target_pairs={{0,8},{8,0},{16,24},{24,16},{1,9},{9,1},{17,25},{25,17},{2,10},{10... | collective-permute-start | bytes 589832 | tf_op jit(solution)/shard_map/ppermute | solution.py:408
  157.8 10.8 %collective-permute-start.33 = (f32[64,768]{1,0:T(8,128)S(1)}, f32[64,768]{1,0:T(8,128)S(1)}, u32[]{:S(2)}, u32[]{:S(2)}) collective-permute-start(f32[64,768]{1,0:T(8,128)S(1)} %over_z.3.refs_4_), channel_id=1, source_target_pairs={{0,16},{8,24},{16,0},{24,8},{1,17},{9,25},{17,1},{25,9},{2,18},{10... | collective-permute-start | bytes 589832 | tf_op jit(solution)/shard_map/ppermute | solution.py:408
  158.6 9.9 %collective-permute-start.34 = (f32[64,768]{1,0:T(8,128)S(1)}, f32[64,768]{1,0:T(8,128)S(1)}, u32[]{:S(2)}, u32[]{:S(2)}) collective-permute-start(f32[64,768]{1,0:T(8,128)S(1)} %over_z.3.refs_4_), channel_id=1, source_target_pairs={{0,24},{8,16},{16,8},{24,0},{1,25},{9,17},{17,9},{25,1},{2,26},{10... | collective-permute-start | bytes 589832 | tf_op jit(solution)/shard_map/ppermute | solution.py:408
  (33 other events, 132.6 us)
where the time goes:
time: 171 us; the launch traced here: 170 us
  waiting for transfers between devices  55.8 us (33%)
  starting transfers between devices  51.9 us (30%)
  Pallas kernels  44.7 us (26%)
  local copies, waits for them, and re-layouts  16 us (9%)
    ppermute x16, waiting for transfers between devices, swap_t(): return lax.ppermute(value, 'teacher', [(t, t ^ k) for t in range(n_t)])  24.9 us
    ppermute x16, starting transfers between devices, swap_t(): return lax.ppermute(value, 'teacher', [(t, t ^ k) for t in range(n_t)])  20.6 us
    unnamed x54, local copies, waits for them, and re-layouts  16 us
    ppermute x9, starting transfers between devices, swap_z(): return lax.ppermute(value, 'dp', [(d, d ^ 2 * k) for d in range(n_dp)])  16 us
    pallas_call x1, Pallas kernels, ffn(): call(functools.partial(ffn_kernel, slice_w, n), 'ffn', [shape((frames, w)...  14.3 us
    all_to_all x1, waiting for transfers between devices, body(): lax.all_to_all(h_out, 'teacher', split_axis=0, concat_axis=0, tiled=True)  13.2 us
    ppermute x9, waiting for transfers between devices, swap_z(): return lax.ppermute(value, 'dp', [(d, d ^ 2 * k) for d in range(n_dp)])  12 us
    pallas_call x1, Pallas kernels, backward(): call(functools.partial(backward_kernel, (n_t, n_z, rows, out_rows, slice_...  7.56 us
  transfers between devices with their start and end apart: 38, of which 20 were waited for; matrix products, arithmetic and copies ran while one was open for 0% of the time, Pallas kernels for 14%

commit v1 on v0

--- a/solution.py
+++ b/solution.py
@@ -13,6 +13,7 @@
 I32 = jnp.int32
 BLK = 256
 FFN_MB = 50
+STUDENT_MB = 44
 VMEM = pl.BlockSpec(memory_space=pltpu.VMEM)
 SMEM = pl.BlockSpec(memory_space=pltpu.SMEM)
 ANY = pl.BlockSpec(memory_space=pl.ANY)
@@ -134,14 +135,15 @@
     copy_all(pairs, sem)
 
 
-def halves_kernel(from_x, from_y, to_y, to_x, sem):
+def halves_kernel(from_x, from_y, *refs):
+    to_y, to_x, sem = refs[-3:]
     half = to_x.shape[0]
     copy_all([(from_x.at[pl.ds(half, half), :], to_y), (from_y.at[pl.ds(0, half), :], to_x)], sem)
 
 
 def ffn_kernel(slice_w, n, *refs):
-    h_refs, w_refs, after, e_refs = refs[:n], refs[n : n + 6], refs[n + 6], refs[n + 7 : n + 10]
-    hid, w_bufs, e_bufs, normed, sem = refs[n + 10], refs[n + 11 : n + 17], e_refs, refs[n + 17], refs[n + 18]
+    h_refs, w_refs, refs = refs[:n], refs[n : n + 6], refs[-12:]
+    e_bufs, hid, w_bufs, (normed, sem) = refs[:3], refs[3], refs[4:10], refs[10:]
     me = lax.axis_index("teacher")
     frames = hid.shape[0]
     half = frames // 2
@@ -186,38 +188,50 @@
         functools.partial(ffn_kernel, slice_w, n),
         "ffn",
         [shape((frames, w), F32) for w in widths],
-        [HBM] * (n + 6) + [ANY],
+        [HBM] * (n + 6) + [ANY] * len(after),
         scratch=[pltpu.VMEM((frames, wall), BF)]
         + [pltpu.VMEM(w.shape, BF) for w in weights]
         + [pltpu.VMEM((frames, max(widths)), BF), pltpu.SemaphoreType.DMA((n + 6,))],
         limit=FFN_MB,
         us=13,
-    )(*pieces, *weights, after)
-
-
-def forward_kernel(dims, *refs):
-    n_t, n_z, rows, out_rows, slice_w = dims
-    s_ref, w_refs, h_refs, refs = refs[0], refs[1 : 1 + 2 * n_z], refs[1 + 2 * n_z : 3 + 2 * n_z], refs[3 + 2 * n_z + n_t - 1 :]
-    e_refs, (act, slope, w_out, err, keep, send), (w_in, w_head, pred, sem) = refs[:3], refs[3:9], refs[9:]
+    )(*pieces, *weights, *after)
+
+
+def student_kernel(dims, *refs):
+    n_t, n_z, rows, out_rows = dims
+    s_ref, w_refs, h_refs, refs = refs[0], refs[1 : 1 + 2 * n_z], refs[1 + 2 * n_z : 1 + 2 * n_z + 2 * n_t], refs[-19:]
+    e_hbm, (h_keep, h_send, keep, send) = refs[:3], refs[3:7]
+    w_in, w_out, w_head, pred, act, slope, err, student_t, *e_refs, sem = refs[7:]
     me_t = lax.axis_index("teacher")
     me_d = lax.axis_index("dp")
     z, core = me_d // 2, me_d % 2
     sd, sff = w_in.shape
+    slice_w = w_head.shape[1] // n_t
+    half_w = slice_w // 2
     parts = out_rows // rows
     pairs = []
     for i in range(2 * n_z):
-        shard = 2 * (z ^ (i // 2)) + (core if i % 2 == 0 else 1 - core)
+        shard = 2 * lax.rem(z + n_z - i // 2, n_z) + (core if i % 2 == 0 else 1 - core)
         src = w_refs[i]
         pairs.append((src.at[:, pl.ds(0, sff)], w_in.at[aligned(shard, rows, 16), :]))
         for p in range(parts):
             at = pl.multiple_of(shard * out_rows + p * rows, 16)
             pairs.append((src.at[:, pl.ds(sff + p * sd, sd)], w_out.at[pl.ds(at, rows), :]))
-    for c in range(2):
-        pairs.append((h_refs[c], w_head.at[:, aligned(core if c == 0 else 1 - core, slice_w // 2, 128)]))
-    copy_all(pairs, sem)
+    first = len(pairs)
+    for k in range(n_t):
+        for c in range(2):
+            at = (me_t ^ k) * slice_w + (core if c == 0 else 1 - core) * half_w
+            pairs.append((h_refs[2 * k + c], w_head.at[:, pl.ds(pl.multiple_of(at, 128), half_w)]))
+    pairs += list(zip(e_hbm, e_refs))
+    copies = [pltpu.make_async_copy(a, b, sem.at[i]) for i, (a, b) in enumerate(pairs)]
+    for c in copies:
+        c.start()
     order = [me_t ^ k for k in range(n_t)]
     student = jnp.concatenate([s_ref[k, :, pl.ds(0, sd)] for k in order], axis=0)
     mask = jnp.concatenate([s_ref[k, :, pl.ds(sd, 128)] for k in order], axis=0).astype(F32)
+    student_t[...] = student.T
+    for c in copies[:first]:
+        c.wait()
     total = student.astype(F32)
     for b in range(0, sff, BLK):
         pre = dot(student, w_in[:, pl.ds(b, BLK)])
@@ -230,7 +244,9 @@
         total = total + dot(swoosh, w_out[pl.ds(b, BLK), :])
     features = total.astype(BF)
     feat_t = features.T
-    pred[...] = dot(features, w_head[...])
+    for c in copies[first:]:
+        c.wait()
+    pred[...] = dot(features, w_head[:, aligned(me_t, slice_w, 128)])
 
     at = 0
     for ref in e_refs:
@@ -245,68 +261,18 @@
             err[:, pl.ds(col, BLK)] = value
             product = dot(feat_t, value)
             for i in range(n_z):
-                pair = product[2 * i * rows : 2 * (i + 1) * rows]
-                low, high = pair[:rows], pair[rows:]
-                keep[i, :, pl.ds(col, BLK)] = jnp.where(core == 0, low, high)
-                send[i, :, pl.ds(col, BLK)] = jnp.where(core == 0, high, low).astype(BF)
+                low, high = product[2 * i * rows : (2 * i + 1) * rows], product[(2 * i + 1) * rows : 2 * (i + 1) * rows]
+                h_keep[i, :, pl.ds(col, BLK)] = jnp.where(core == 0, low, high)
+                h_send[i, :, pl.ds(col, BLK)] = jnp.where(core == 0, high, low).astype(BF)
         at += width
 
-
-def forward(s_all, w_pieces, h_pieces, after, e_parts, n_z, rows, out_rows, slice_w, sff):
-    n_t, frames, sd = s_all.shape
-    frames, sd = n_t * frames, sd - 128
-    wall = sum(e.shape[1] for e in e_parts)
-    return call(
-        functools.partial(forward_kernel, (n_t, n_z, rows, out_rows, slice_w)),
-        "student_forward",
-        [
-            shape((frames, sff), BF),
-            shape((frames, sff), F32),
-            shape((sff, sd), BF),
-            shape((frames, wall), BF),
-            shape((n_z, rows, wall), F32),
-            shape((n_z, rows, wall), BF),
-        ],
-        [VMEM] + [ANY] * (2 * n_z + 2 + n_t - 1) + [VMEM] * 3,
-        scratch=[
-            pltpu.VMEM((sd, sff), BF),
-            pltpu.VMEM((sd, slice_w), BF),
-            pltpu.VMEM((frames, slice_w), F32),
-        ]
-        + [pltpu.SemaphoreType.DMA((2 * n_z * (1 + out_rows // rows) + 2,))],
-        limit=16,
-        us=7,
-    )(s_all, *w_pieces, *h_pieces, *after, *e_parts)
-
-
-def backward_kernel(dims, *refs):
-    n_t, n_z, rows, out_rows, slice_w = dims
-    s_ref, h_refs = refs[0], refs[1 : 1 + 2 * n_t]
-    err, act, slope, w_out, after, keep, send, w_head, student_t, sem = refs[1 + 2 * n_t :]
-    me_t = lax.axis_index("teacher")
-    me_d = lax.axis_index("dp")
-    z, core = me_d // 2, me_d % 2
-    copies = []
-    for k in range(n_t):
-        for c in range(2):
-            at = (me_t ^ k) * slice_w + (core if c == 0 else 1 - core) * (slice_w // 2)
-            dst = w_head.at[:, pl.ds(pl.multiple_of(at, 128), slice_w // 2)]
-            copies.append(pltpu.make_async_copy(h_refs[2 * k + c], dst, sem.at[len(copies)]))
-    for c in copies:
-        c.start()
-    sd = w_head.shape[0]
-    student = jnp.concatenate([s_ref[me_t ^ k, :, pl.ds(0, sd)] for k in range(n_t)], axis=0)
-    student_t[...] = student.T
-    for c in copies:
-        c.wait()
     fg = dot(err[...], w_head[...], ((1,), (1,))).astype(BF)
-    sff = act.shape[1]
     block = sff // 4
     zs = block // (2 * out_rows)
     for b in range(4):
         part = dot(act[:, pl.ds(b * block, block)].T, fg)
         for i in range(zs):
-            for p in range(out_rows // rows):
+            for p in range(parts):
                 at = 2 * i * out_rows + p * rows
                 low, high = part[at : at + rows], part[at + out_rows : at + out_rows + rows]
                 lanes = pl.ds(p * sd, sd)
@@ -316,31 +282,42 @@
         pre_grad = (back * slope[:, pl.ds(b * block, block)]).astype(BF)
         part = dot(student_t[...], pre_grad)
         for i in range(n_z):
-            low = part[2 * i * rows : (2 * i + 1) * rows]
-            high = part[(2 * i + 1) * rows : (2 * i + 2) * rows]
-            lanes = pl.ds(out_rows // rows * sd + b * block, block)
+            low, high = part[2 * i * rows : (2 * i + 1) * rows], part[(2 * i + 1) * rows : (2 * i + 2) * rows]
+            lanes = pl.ds(parts * sd + b * block, block)
             keep[i, :, lanes] = jnp.where(core == 0, low, high)
             send[i, :, lanes] = jnp.where(core == 0, high, low).astype(BF)
 
 
-def backward(s_all, h_pieces, err, act, slope, w_out, after, n_z, rows, out_rows, slice_w):
-    n_t = s_all.shape[0]
-    frames, wall = err.shape
-    sff, sd = w_out.shape
+def student_step(s_all, w_pieces, h_pieces, e_parts, n_z, rows, out_rows, sff):
+    n_t, frames, sd = s_all.shape
+    frames, sd = n_t * frames, sd - 128
+    wall = sum(e.shape[1] for e in e_parts)
     wide = out_rows // rows * sd + sff
     return call(
-        functools.partial(backward_kernel, (n_t, n_z, rows, out_rows, slice_w)),
-        "student_backward",
-        [shape((n_z, rows, wide), F32), shape((n_z, rows, wide), BF)],
-        [VMEM] + [ANY] * (2 * n_t) + [VMEM] * 4 + [ANY],
+        functools.partial(student_kernel, (n_t, n_z, rows, out_rows)),
+        "student",
+        [
+            shape((n_z, rows, wall), F32),
+            shape((n_z, rows, wall), BF),
+            shape((n_z, rows, wide), F32),
+            shape((n_z, rows, wide), BF),
+        ],
+        [VMEM] + [ANY] * (2 * n_z + 2 * n_t) + [HBM] * 3,
         scratch=[
+            pltpu.VMEM((sd, sff), BF),
+            pltpu.VMEM((sff, sd), BF),
             pltpu.VMEM((sd, wall), BF),
+            pltpu.VMEM((frames, wall // n_t), F32),
+            pltpu.VMEM((frames, sff), BF),
+            pltpu.VMEM((frames, sff), F32),
+            pltpu.VMEM((frames, wall), BF),
             pltpu.VMEM((sd, frames), BF),
-            pltpu.SemaphoreType.DMA((2 * n_t,)),
-        ],
-        limit=16,
-        us=6,
-    )(s_all, *h_pieces, err, act, slope, w_out, after)
+        ]
+        + [pltpu.VMEM(e.shape, F32) for e in e_parts]
+        + [pltpu.SemaphoreType.DMA((2 * n_z * (1 + out_rows // rows) + 2 * n_t + 3,))],
+        limit=STUDENT_MB,
+        us=14,
+    )(s_all, *w_pieces, *h_pieces, *e_parts)
 
 
 def add_kernel(own, *refs):
@@ -407,6 +384,9 @@
     def swap_t(k, value):
         return lax.ppermute(value, "teacher", [(t, t ^ k) for t in range(n_t)])
 
+    def shift_z(k, value):
+        return lax.ppermute(value, "dp", [(d, (d + 2 * k) % n_dp) for d in range(n_dp)])
+
     def swap_z(k, value):
         return lax.ppermute(value, "dp", [(d, d ^ (2 * k)) for d in range(n_dp)])
 
@@ -433,32 +413,35 @@
             merge_kernel, "merge", [shape((rows, sff + parts * sd), BF), shape((frames, wall), BF)],
             [HBM] * 5 + [ANY], scratch=[pltpu.SemaphoreType.DMA((parts + 4,))], limit=60,
         )(w_in, w_out, hid_whisper, hid_beats, hid_wavlm, packed)
-        from_z = [merged] + [swap_z(k, merged) for k in range(1, n_z)]
-
         from_x, from_y = swap_t(1, hid), swap_t(2, hid)
         to_y, to_x = call(
             halves_kernel, "halves", [shape((half, wall), BF)] * 2, [HBM] * 2,
-            scratch=[pltpu.SemaphoreType.DMA((2,))], limit=60,
+            scratch=[pltpu.SemaphoreType.DMA((2,))], limit=4,
         )(from_x, from_y)
         group = [hid, from_x, from_y, swap_t(1, to_x), swap_t(2, to_y)]
+        from_z = [merged]
+        for k in range(1, n_z):
+            value = from_z[-1]
+            if k == 2:
+                value, *group = lax.optimization_barrier((value, *group))
+            from_z.append(shift_z(1, value))
 
         s_own, head = call(
             functools.partial(unpack_kernel, n_dp, cap), "unpack",
-            [shape((n_t, frames, sd + 128), BF), shape((sd, slice_w // 2), BF)], [SMEM, SMEM, VMEM], limit=60,
+            [shape((n_t, frames, sd + 128), BF), shape((sd, slice_w // 2), BF)], [SMEM, SMEM, VMEM], limit=8,
         )(send_counts, clip_len, arrived)
         s_all = lax.all_to_all(s_own, "teacher", split_axis=0, concat_axis=0, tiled=True)
         h_mine = [head] + [swap_t(k, head) for k in range(1, n_t)]
-        e_parts = ffn(group, (up_whisper, down_whisper, up_beats, down_beats, up_wavlm, down_wavlm), slice_w, s_own)
-        from_z, h_mine, _ = lax.optimization_barrier((from_z, h_mine, e_parts[0]))
+        e_parts = ffn(group, (up_whisper, down_whisper, up_beats, down_beats, up_wavlm, down_wavlm), slice_w, (s_own, from_z[-2]))
+        from_z, h_mine, s_all, _ = lax.optimization_barrier((from_z, h_mine, s_all, e_parts[0]))
         w_pieces, h_pieces = [], []
         for piece in from_z:
             w_pieces += [piece, swap_core(piece)]
         for piece in h_mine:
             h_pieces += [piece, swap_core(piece)]
 
-        act, slope, full_out, err, h_keep, h_send = forward(
-            s_all, w_pieces, h_pieces[:2], h_mine[1:], e_parts, n_z, rows, out_rows, slice_w, sff
-        )
+        h_keep, h_send, keep, send = student_step(s_all, w_pieces, h_pieces, e_parts, n_z, rows, out_rows, sff)
+
         def chip_sum(keep, send, splits, many):
             chunk = keep.shape[2] // n_t
             sends = [shape((n_z, rows, chunk), BF)] * (n_t - 1) if many else [shape((n_t, n_z, rows, chunk), BF)]
@@ -477,13 +460,12 @@
             total = call(add_kernel, "over_z", shape((rows, chunk), F32), [VMEM] * n_z)(own, *got)
             return [total] + [swap_t(k, total) for k in range(1, n_t)]
 
-        h_own, h_out = chip_sum(h_keep, h_send, [(0, wall)], False)
-        h_got = lax.all_to_all(h_out, "teacher", split_axis=0, concat_axis=0, tiled=True)
-        keep, send = backward(s_all, h_pieces, err, act, slope, full_out, h_own, n_z, rows, out_rows, slice_w)
+        h_own, *h_sends = chip_sum(h_keep, h_send, [(0, wall)], True)
+        h_got = [swap_t(k + 1, v) for k, v in enumerate(h_sends)]
         splits = [(p * sd, sd) for p in range(parts)] + [(parts * sd, sff)]
         r_own, *r_sends = chip_sum(keep, send, splits, True)
         r_got = [swap_t(k + 1, v) for k, v in enumerate(r_sends)]
-        h_all = z_sum(h_own, [h_got])
+        h_all = z_sum(h_own, h_got)
         r_all = z_sum(r_own, r_got)
         grad_in, grad_out, grad_head = call(
             functools.partial(last_kernel, n_t), "last",

time: 171 us -> 158 us (0.924)
  local copies, waits for them, and re-layouts: 16 us -> 5.43 us
  waiting for transfers between devices: 55.8 us -> 64.6 us
  Pallas kernels: 44.7 us -> 38 us
  starting transfers between devices: 51.9 us -> 48.4 us
    all_to_all x1 -> x0, waiting for transfers between devices: 13.2 us -> none  [body(): lax.all_to_all(h_out, 'teacher', split_axis=0, concat_axis=0, tiled=True)]
    ppermute x0 -> x3, waiting for transfers between devices: none -> 10.8 us  [shift_z(): lax.ppermute(value, 'dp', [(d, (d + 2 * k) % n_dp) for d in range(n_dp)])]
    unnamed x54 -> x20, local copies, waits for them, and re-layouts: 16 us -> 5.43 us
    ppermute x16 -> x19, waiting for transfers between devices: 24.9 us -> 34.5 us  [swap_t(): return lax.ppermute(value, 'teacher', [(t, t ^ k) for t in range(n_t)])]
    ppermute x9 -> x6, starting transfers between devices: 16 us -> 8.68 us  [swap_z(): return lax.ppermute(value, 'dp', [(d, d ^ 2 * k) for d in range(n_dp)])]
    ppermute x16 -> x19, starting transfers between devices: 20.6 us -> 25.6 us  [swap_t(): return lax.ppermute(value, 'teacher', [(t, t ^ k) for t in range(n_t)])]
    all_to_all x1 -> x0, starting transfers between devices: 4.58 us -> none  [body(): lax.all_to_all(h_out, 'teacher', split_axis=0, concat_axis=0, tiled=True)]
    ppermute x0 -> x3, starting transfers between devices: none -> 3.55 us  [shift_z(): lax.ppermute(value, 'dp', [(d, (d + 2 * k) % n_dp) for d in range(n_dp)])]
  transfers between devices with their start and end apart: 38 -> 40, of which waited for: 20 -> 23; matrix products, arithmetic and copies ran while one was open for 0% -> 0% of each run, Pallas kernels for 14% -> 11%
where the time goes in v1:
time: 158 us
  waiting for transfers between devices  64.6 us (41%)
  starting transfers between devices  48.4 us (31%)
  Pallas kernels  38 us (24%)
  local copies, waits for them, and re-layouts  5.43 us (3%)
    ppermute x19, waiting for transfers between devices, swap_t(): return lax.ppermute(value, 'teacher', [(t, t ^ k) for t in range(n_t)])  34.5 us
    ppermute x19, starting transfers between devices, swap_t(): return lax.ppermute(value, 'teacher', [(t, t ^ k) for t in range(n_t)])  25.6 us
    pallas_call x1, Pallas kernels, ffn(): call(functools.partial(ffn_kernel, slice_w, n), 'ffn', [shape((frames, w)...  14.3 us
    pallas_call x1, Pallas kernels, student_step(): call(functools.partial(student_kernel, (n_t, n_z, rows, out_rows)), 'stud...  14.2 us
    ppermute x6, waiting for transfers between devices, swap_z(): return lax.ppermute(value, 'dp', [(d, d ^ 2 * k) for d in range(n_dp)])  11.4 us
    ppermute x3, waiting for transfers between devices, shift_z(): lax.ppermute(value, 'dp', [(d, (d + 2 * k) % n_dp) for d in range(n_dp)])  10.8 us
    ppermute x6, starting transfers between devices, swap_z(): return lax.ppermute(value, 'dp', [(d, d ^ 2 * k) for d in range(n_dp)])  8.68 us
    ppermute x10, waiting for transfers between devices, swap_core(): return lax.ppermute(value, 'dp', [(d, d ^ 1) for d in range(n_dp)])  7.1 us
  transfers between devices with their start and end apart: 40, of which 23 were waited for; matrix products, arithmetic and copies ran while one was open for 0% of the time, Pallas kernels for 11%

profile of v1, /device:TPU:0, one launch (start us, length us, event | category | flops | bytes accessed | tf_op | source)
XLA Modules:
  0.0 157.9 jit_solution(15129977014919921241)
XLA Ops:
  0.6 2.3 %pack.1.after = bf16[512,640]{1,0:T(8,128)(2,1)} custom-call(s32[1,8,8]{2,1,0:T(8,128)} %table.3, bf16[128,512]{1,0:T(8,128)(2,1)} %student.2, bf16[64,3072]{1,0:T(8,128)(2,1)} %w_head.1), custom_call_target="tpu_custom_call" | custom-call | flops 1000000000 | bytes 3000000 | tf_op jit(solution)/shard_map/pack/pallas_call | solution.py:406
  2.9 2.4 %merge.1 = (bf16[64,3072]{1,0:T(8,128)(2,1)}, bf16[128,3072]{1,0:T(8,128)(2,1)}) custom-call(bf16[64,1536]{1,0:T(8,128)(2,1)} %w_in.1, bf16[192,512]{1,0:T(8,128)(2,1)} %w_out.1, bf16[128,1280]{1,0:T(8,128)(2,1)} %whisper.1, bf16[128,768]{1,0:T(8,128)(2,1)} %beats.1, bf16[128,1024]{1,0:T(8,128)(2,1)} %wavlm.1, bf16[512,640]{1,0:T(8,128)(2,1)} %pack.1.after), custom_call_target="tpu_custom_call" | custom-call | flops 1000000000 | bytes 3000000 | tf_op jit(solution)/shard_map/merge/pallas_call | solution.py:412
  5.3 3.0 %collective-permute-start.2 = (bf16[128,3072]{1,0:T(8,128)(2,1)}, bf16[128,3072]{1,0:T(8,128)(2,1)S(1)}, u32[]{:S(2)}, u32[]{:S(2)}) collective-permute-start(bf16[128,3072]{1,0:T(8,128)(2,1)} %get-tuple-element.54.refs_0_), channel_id=1, source_target_pairs={{0,16},{8,24},{16,0},{24,8},{1,17},{9,25},{17,1},{25,9},{2,18},{10... | collective-permute-start | bytes 2359304 | tf_op jit(solution)/shard_map/ppermute | solution.py:385
  8.3 1.5 collective-permute-start.1
  9.8 4.9 %all-to-all-start = ((bf16[8,64,640]{2,1,0:T(8,128)(2,1)}), bf16[8,64,640]{2,1,0:T(8,128)(2,1)S(1)}, u32[]{:S(2)}, u32[]{:S(2)}) async-start(bf16[8,64,640]{2,1,0:T(8,128)(2,1)} %bitcast), calls=%async_computation | async-start | bytes 1310720 | tf_op jit(solution)/shard_map/all_to_all | solution.py:410
  14.7 2.0 %collective-permute-start = (bf16[64,3072]{1,0:T(8,128)(2,1)}, bf16[64,3072]{1,0:T(8,128)(2,1)S(1)}, u32[]{:S(2)}, u32[]{:S(2)}) collective-permute-start(bf16[64,3072]{1,0:T(8,128)(2,1)} %get-tuple-element.61.refs_1_), channel_id=1, source_target_pairs={{0,2},{1,3},{2,4},{3,5},{4,6},{5,7},{6,0},{7,1},{8,10},{9,11},{10,... | collective-permute-start | bytes 1179656 | tf_op jit(solution)/shard_map/ppermute | solution.py:388
  16.7 9.4 %collective-permute-done.2.from_y.refs_2_ = bf16[128,3072]{1,0:T(8,128)(2,1)S(1)} collective-permute-done((bf16[128,3072]{1,0:T(8,128)(2,1)}, bf16[128,3072]{1,0:T(8,128)(2,1)S(1)}, u32[]{:S(2)}, u32[]{:S(2)}) %collective-permute-start.2) | collective-permute-done | bytes 786464 | tf_op jit(solution)/shard_map/ppermute | solution.py:385
  26.1 1.5 collective-permute-done.1.from_x.refs_1_
  27.9 1.6 collective-permute-start.3
  30.0 8.8 %collective-permute-done.refs_3_ = bf16[64,3072]{1,0:T(8,128)(2,1)S(1)} collective-permute-done((bf16[64,3072]{1,0:T(8,128)(2,1)}, bf16[64,3072]{1,0:T(8,128)(2,1)S(1)}, u32[]{:S(2)}, u32[]{:S(2)}) %collective-permute-start) | collective-permute-done | bytes 393248 | tf_op jit(solution)/shard_map/ppermute | solution.py:388
  42.1 1.8 %unpack.1 = (bf16[4,128,640]{2,1,0:T(8,128)(2,1)}, bf16[512,384]{1,0:T(8,128)(2,1)}) custom-call(s32[1,8,8]{2,1,0:T(8,128)S(1)} %copy-done.9, s32[1]{0:T(128)S(6)} %copy.18.clip_len, bf16[512,640]{1,0:T(8,128)(2,1)S(1)} %bitcast.2), custom_call_target="tpu_custom_call" | custom-call | flops 1000000000 | bytes 3000000 | tf_op jit(solution)/shard_map/unpack/pallas_call | solution.py:429
  47.3 3.5 %all-to-all-start.1 = ((bf16[4,128,640]{2,1,0:T(8,128)(2,1)}), bf16[4,128,640]{2,1,0:T(8,128)(2,1)S(1)}, u32[]{:S(2)}, u32[]{:S(2)}) async-start(bf16[4,128,640]{2,1,0:T(8,128)(2,1)} %get-tuple-element.53.refs_11_), calls=%async_computation.1 | async-start | bytes 1310720 | tf_op jit(solution)/shard_map/all_to_all | solution.py:433
  50.9 2.0 %collective-permute-done.5.refs_12_.refs_5_ = bf16[64,3072]{1,0:T(8,128)(2,1)} collective-permute-done((bf16[64,3072]{1,0:T(8,128)(2,1)S(1)}, bf16[64,3072]{1,0:T(8,128)(2,1)}, u32[]{:S(2)}, u32[]{:S(2)}) %collective-permute-start.5) | collective-permute-done | bytes 393248 | tf_op jit(solution)/shard_map/ppermute | solution.py:388
  55.3 14.3 %ffn.1 = (f32[512,1280]{1,0:T(8,128)}, f32[512,768]{1,0:T(8,128)}, f32[512,1024]{1,0:T(8,128)}) custom-call(bf16[128,3072]{1,0:T(8,128)(2,1)S(1)} %copy-done.2, bf16[128,3072]{1,0:T(8,128)(2,1)S(1)} %collective-permute-done.1.from_x.refs_1_, bf16[128,3072]{1,0:T(8,128)(2,1)} %copy-done.3, bf16[64,3072]{1,0:T(8,128)(2,1)S(1)} %copy-done.6, ...), custom_call_target="tpu_custom_call" | custom-call | flops 12999999488 | bytes 39000000 | tf_op jit(solution)/shard_map/ffn/pallas_call | solution.py:187
  76.4 14.2 %student.3 = (f32[4,64,3072]{2,1,0:T(8,128)}, bf16[4,64,3072]{2,1,0:T(8,128)(2,1)S(1)}, f32[4,64,3072]{2,1,0:T(8,128)}, bf16[4,64,3072]{2,1,0:T(8,128)(2,1)S(1)}) custom-call(bf16[4,128,640]{2,1,0:T(8,128)(2,1)S(1)} %all-to-all-done.1.refs_0_, bf16[64,3072]{1,0:T(8,128)(2,1)S(1)} %copy-done.4, bf16[64,3072]{1,0:T(8,128)(2,1)S(1)} %collective-permute-done.10.refs_2_, ...), custom_call_target="tpu_custom_call" | custom-call | flops 14000000000 | bytes 42000000 | tf_op jit(solution)/shard_map/student/pallas_call | solution.py:296
  91.2 2.9 %collective-permute-done.18.recv = bf16[4,64,3072]{2,1,0:T(8,128)(2,1)S(1)} collective-permute-done((bf16[4,64,3072]{2,1,0:T(8,128)(2,1)S(1)}, bf16[4,64,3072]{2,1,0:T(8,128)(2,1)S(1)}, u32[]{:S(2)}, u32[]{:S(2)}) %collective-permute-start.18) | collective-permute-done | bytes 1572896 | tf_op jit(solution)/shard_map/ppermute | solution.py:394
  94.1 1.9 %copy-done.1 = f32[4,64,3072]{2,1,0:T(8,128)S(1)} copy-done((f32[4,64,3072]{2,1,0:T(8,128)S(1)}, f32[4,64,3072]{2,1,0:T(8,128)}, u32[]{:S(2)}) %copy-start.1) | copy-done | bytes 3145752
  103.2 5.2 %collective-permute-done.19.refs_0_ = bf16[4,64,768]{2,1,0:T(8,128)(2,1)S(1)} collective-permute-done((bf16[4,64,768]{2,1,0:T(8,128)(2,1)S(1)}, bf16[4,64,768]{2,1,0:T(8,128)(2,1)S(1)}, u32[]{:S(2)}, u32[]{:S(2)}) %collective-permute-start.19) | collective-permute-done | bytes 393248 | tf_op jit(solution)/shard_map/ppermute | solution.py:385
  108.4 2.0 %collective-permute-start.31 = (bf16[4,64,768]{2,1,0:T(8,128)(2,1)S(1)}, bf16[4,64,768]{2,1,0:T(8,128)(2,1)S(1)}, u32[]{:S(2)}, u32[]{:S(2)}) collective-permute-start(bf16[4,64,768]{2,1,0:T(8,128)(2,1)S(1)} %get-tuple-element.86), channel_id=1, source_target_pairs={{0,24},{8,16},{16,8},{24,0},{1,25},{9,17},{17,9},{25,1},{2,26},{10... | collective-permute-start | bytes 1179656 | tf_op jit(solution)/shard_map/ppermute | solution.py:385
  110.4 7.7 %collective-permute-done.20.refs_1_ = bf16[4,64,768]{2,1,0:T(8,128)(2,1)S(1)} collective-permute-done((bf16[4,64,768]{2,1,0:T(8,128)(2,1)S(1)}, bf16[4,64,768]{2,1,0:T(8,128)(2,1)S(1)}, u32[]{:S(2)}, u32[]{:S(2)}) %collective-permute-start.20) | collective-permute-done | bytes 393248 | tf_op jit(solution)/shard_map/ppermute | solution.py:385
  118.3 2.4 %collective-permute-start.22 = (bf16[64,768]{1,0:T(8,128)(2,1)S(1)}, bf16[64,768]{1,0:T(8,128)(2,1)S(1)}, u32[]{:S(2)}, u32[]{:S(2)}) collective-permute-start(bf16[64,768]{1,0:T(8,128)(2,1)S(1)} %get-tuple-element.78), channel_id=1, source_target_pairs={{0,2},{1,3},{2,0},{3,1},{4,6},{5,7},{6,4},{7,5},{8,10},{9,11},{10,... | collective-permute-start | bytes 294920 | tf_op jit(solution)/shard_map/ppermute | solution.py:391
  121.2 3.2 %collective-permute-done.22.refs_0_ = bf16[64,768]{1,0:T(8,128)(2,1)S(1)} collective-permute-done((bf16[64,768]{1,0:T(8,128)(2,1)S(1)}, bf16[64,768]{1,0:T(8,128)(2,1)S(1)}, u32[]{:S(2)}, u32[]{:S(2)}) %collective-permute-start.22) | collective-permute-done | bytes 98336 | tf_op jit(solution)/shard_map/ppermute | solution.py:391
  125.3 3.5 %collective-permute-done.23.refs_1_ = bf16[64,768]{1,0:T(8,128)(2,1)S(1)} collective-permute-done((bf16[64,768]{1,0:T(8,128)(2,1)S(1)}, bf16[64,768]{1,0:T(8,128)(2,1)S(1)}, u32[]{:S(2)}, u32[]{:S(2)}) %collective-permute-start.23) | collective-permute-done | bytes 98336 | tf_op jit(solution)/shard_map/ppermute | solution.py:391
  128.8 2.1 %collective-permute-done.24.refs_2_ = bf16[64,768]{1,0:T(8,128)(2,1)S(1)} collective-permute-done((bf16[64,768]{1,0:T(8,128)(2,1)S(1)}, bf16[64,768]{1,0:T(8,128)(2,1)S(1)}, u32[]{:S(2)}, u32[]{:S(2)}) %collective-permute-start.24) | collective-permute-done | bytes 98336 | tf_op jit(solution)/shard_map/ppermute | solution.py:391
  130.9 1.6 %collective-permute-start.27 = (f32[64,768]{1,0:T(8,128)S(1)}, f32[64,768]{1,0:T(8,128)S(1)}, u32[]{:S(2)}, u32[]{:S(2)}) collective-permute-start(f32[64,768]{1,0:T(8,128)S(1)} %over_z.2.refs_0_), channel_id=1, source_target_pairs={{0,24},{8,16},{16,8},{24,0},{1,25},{9,17},{17,9},{25,1},{2,26},{10... | collective-permute-start | bytes 589832 | tf_op jit(solution)/shard_map/ppermute | solution.py:385
  132.5 5.5 %collective-permute-done.30.refs_1_ = bf16[4,64,768]{2,1,0:T(8,128)(2,1)S(1)} collective-permute-done((bf16[4,64,768]{2,1,0:T(8,128)(2,1)S(1)}, bf16[4,64,768]{2,1,0:T(8,128)(2,1)S(1)}, u32[]{:S(2)}, u32[]{:S(2)}) %collective-permute-start.30) | collective-permute-done | bytes 393248 | tf_op jit(solution)/shard_map/ppermute | solution.py:385
  138.2 2.4 %collective-permute-start.32 = (bf16[64,768]{1,0:T(8,128)(2,1)S(1)}, bf16[64,768]{1,0:T(8,128)(2,1)S(1)}, u32[]{:S(2)}, u32[]{:S(2)}) collective-permute-start(bf16[64,768]{1,0:T(8,128)(2,1)S(1)} %get-tuple-element.88), channel_id=1, source_target_pairs={{0,2},{1,3},{2,0},{3,1},{4,6},{5,7},{6,4},{7,5},{8,10},{9,11},{10,... | collective-permute-start | bytes 294920 | tf_op jit(solution)/shard_map/ppermute | solution.py:391
  141.1 2.0 %collective-permute-start.34 = (bf16[64,768]{1,0:T(8,128)(2,1)S(1)}, bf16[64,768]{1,0:T(8,128)(2,1)S(1)}, u32[]{:S(2)}, u32[]{:S(2)}) collective-permute-start(bf16[64,768]{1,0:T(8,128)(2,1)S(1)} %get-tuple-element.90), channel_id=1, source_target_pairs={{0,6},{1,7},{2,4},{3,5},{4,2},{5,3},{6,0},{7,1},{8,14},{9,15},{10,... | collective-permute-start | bytes 294920 | tf_op jit(solution)/shard_map/ppermute | solution.py:391
  145.2 2.6 %collective-permute-done.33.refs_1_ = bf16[64,768]{1,0:T(8,128)(2,1)S(1)} collective-permute-done((bf16[64,768]{1,0:T(8,128)(2,1)S(1)}, bf16[64,768]{1,0:T(8,128)(2,1)S(1)}, u32[]{:S(2)}, u32[]{:S(2)}) %collective-permute-start.33) | collective-permute-done | bytes 98336 | tf_op jit(solution)/shard_map/ppermute | solution.py:391
  147.9 1.6 %collective-permute-start.37 = (f32[64,768]{1,0:T(8,128)S(1)}, f32[64,768]{1,0:T(8,128)S(1)}, u32[]{:S(2)}, u32[]{:S(2)}) collective-permute-start(f32[64,768]{1,0:T(8,128)S(1)} %over_z.3.refs_4_), channel_id=1, source_target_pairs={{0,24},{8,16},{16,8},{24,0},{1,25},{9,17},{17,9},{25,1},{2,26},{10... | collective-permute-start | bytes 589832 | tf_op jit(solution)/shard_map/ppermute | solution.py:385
  151.6 3.0 %collective-permute-done.37.refs_7_ = f32[64,768]{1,0:T(8,128)S(1)} collective-permute-done((f32[64,768]{1,0:T(8,128)S(1)}, f32[64,768]{1,0:T(8,128)S(1)}, u32[]{:S(2)}, u32[]{:S(2)}) %collective-permute-start.37) | collective-permute-done | bytes 196640 | tf_op jit(solution)/shard_map/ppermute | solution.py:385
  154.6 2.0 %collective-permute-done.36.refs_6_ = f32[64,768]{1,0:T(8,128)S(1)} collective-permute-done((f32[64,768]{1,0:T(8,128)S(1)}, f32[64,768]{1,0:T(8,128)S(1)}, u32[]{:S(2)}, u32[]{:S(2)}) %collective-permute-start.36) | collective-permute-done | bytes 196640 | tf_op jit(solution)/shard_map/ppermute | solution.py:385
  (81 shorter events, 31.7 us)
Async XLA Ops:
  5.3 20.8 %collective-permute-start.2 = (bf16[128,3072]{1,0:T(8,128)(2,1)}, bf16[128,3072]{1,0:T(8,128)(2,1)S(1)}, u32[]{:S(2)}, u32[]{:S(2)}) collective-permute-start(bf16[128,3072]{1,0:T(8,128)(2,1)} %get-tuple-element.54.refs_0_), channel_id=1, source_target_pairs={{0,16},{8,24},{16,0},{24,8},{1,17},{9,25},{17,1},{25,9},{2,18},{10... | collective-permute-start | bytes 2359304 | tf_op jit(solution)/shard_map/ppermute | solution.py:385
  8.3 19.2 %collective-permute-start.1 = (bf16[128,3072]{1,0:T(8,128)(2,1)}, bf16[128,3072]{1,0:T(8,128)(2,1)S(1)}, u32[]{:S(2)}, u32[]{:S(2)}) collective-permute-start(bf16[128,3072]{1,0:T(8,128)(2,1)} %get-tuple-element.54.refs_0_), channel_id=1, source_target_pairs={{0,8},{8,0},{16,24},{24,16},{1,9},{9,1},{17,25},{25,17},{2,10},{10... | collective-permute-start | bytes 2359304 | tf_op jit(solution)/shard_map/ppermute | solution.py:385
  9.8 32.2 %all-to-all-start = ((bf16[8,64,640]{2,1,0:T(8,128)(2,1)}), bf16[8,64,640]{2,1,0:T(8,128)(2,1)S(1)}, u32[]{:S(2)}, u32[]{:S(2)}) async-start(bf16[8,64,640]{2,1,0:T(8,128)(2,1)} %bitcast), calls=%async_computation | async-start | bytes 1310720 | tf_op jit(solution)/shard_map/all_to_all | solution.py:410
  14.7 24.1 %collective-permute-start = (bf16[64,3072]{1,0:T(8,128)(2,1)}, bf16[64,3072]{1,0:T(8,128)(2,1)S(1)}, u32[]{:S(2)}, u32[]{:S(2)}) collective-permute-start(bf16[64,3072]{1,0:T(8,128)(2,1)} %get-tuple-element.61.refs_1_), channel_id=1, source_target_pairs={{0,2},{1,3},{2,4},{3,5},{4,6},{5,7},{6,0},{7,1},{8,10},{9,11},{10,... | collective-permute-start | bytes 1179656 | tf_op jit(solution)/shard_map/ppermute | solution.py:388
  27.9 10.9 %collective-permute-start.3 = (bf16[64,3072]{1,0:T(8,128)(2,1)S(1)}, bf16[64,3072]{1,0:T(8,128)(2,1)S(1)}, u32[]{:S(2)}, u32[]{:S(2)}) collective-permute-start(bf16[64,3072]{1,0:T(8,128)(2,1)S(1)} %get-tuple-element.49), channel_id=1, source_target_pairs={{0,8},{8,0},{16,24},{24,16},{1,9},{9,1},{17,25},{25,17},{2,10},{10... | collective-permute-start | bytes 1179656 | tf_op jit(solution)/shard_map/ppermute | solution.py:385
  29.5 10.1 %collective-permute-start.4 = (bf16[64,3072]{1,0:T(8,128)(2,1)S(1)}, bf16[64,3072]{1,0:T(8,128)(2,1)S(1)}, u32[]{:S(2)}, u32[]{:S(2)}) collective-permute-start(bf16[64,3072]{1,0:T(8,128)(2,1)S(1)} %get-tuple-element.50), channel_id=1, source_target_pairs={{0,16},{8,24},{16,0},{24,8},{1,17},{9,25},{17,1},{25,9},{2,18},{10... | collective-permute-start | bytes 1179656 | tf_op jit(solution)/shard_map/ppermute | solution.py:385
  40.3 12.5 %collective-permute-start.5 = (bf16[64,3072]{1,0:T(8,128)(2,1)S(1)}, bf16[64,3072]{1,0:T(8,128)(2,1)}, u32[]{:S(2)}, u32[]{:S(2)}) collective-permute-start(bf16[64,3072]{1,0:T(8,128)(2,1)S(1)} %collective-permute-done.refs_3_), channel_id=1, source_target_pairs={{0,2},{1,3},{2,4},{3,5},{4,6},{5,7},{6,0},{7,1},{8,10},{9,11},{10,... | collective-permute-start | bytes 1179656 | tf_op jit(solution)/shard_map/ppermute | solution.py:388
  43.9 25.7 %collective-permute-start.9 = (bf16[512,384]{1,0:T(8,128)(2,1)}, bf16[512,384]{1,0:T(8,128)(2,1)S(1)}, u32[]{:S(2)}, u32[]{:S(2)}) collective-permute-start(bf16[512,384]{1,0:T(8,128)(2,1)} %get-tuple-element.65.refs_9_), channel_id=1, source_target_pairs={{0,24},{8,16},{16,8},{24,0},{1,25},{9,17},{17,9},{25,1},{2,26},{10... | collective-permute-start | bytes 1179656 | tf_op jit(solution)/shard_map/ppermute | solution.py:385
  44.7 24.9 %collective-permute-start.8 = (bf16[512,384]{1,0:T(8,128)(2,1)}, bf16[512,384]{1,0:T(8,128)(2,1)}, u32[]{:S(2)}, u32[]{:S(2)}) collective-permute-start(bf16[512,384]{1,0:T(8,128)(2,1)} %get-tuple-element.65.refs_9_), channel_id=1, source_target_pairs={{0,16},{8,24},{16,0},{24,8},{1,17},{9,25},{17,1},{25,9},{2,18},{10... | collective-permute-start | bytes 1179656 | tf_op jit(solution)/shard_map/ppermute | solution.py:385
  46.2 23.4 %collective-permute-start.7 = (bf16[512,384]{1,0:T(8,128)(2,1)}, bf16[512,384]{1,0:T(8,128)(2,1)}, u32[]{:S(2)}, u32[]{:S(2)}) collective-permute-start(bf16[512,384]{1,0:T(8,128)(2,1)} %get-tuple-element.65.refs_9_), channel_id=1, source_target_pairs={{0,8},{8,0},{16,24},{24,16},{1,9},{9,1},{17,25},{25,17},{2,10},{10... | collective-permute-start | bytes 1179656 | tf_op jit(solution)/shard_map/ppermute | solution.py:385
  47.3 23.2 %all-to-all-start.1 = ((bf16[4,128,640]{2,1,0:T(8,128)(2,1)}), bf16[4,128,640]{2,1,0:T(8,128)(2,1)S(1)}, u32[]{:S(2)}, u32[]{:S(2)}) async-start(bf16[4,128,640]{2,1,0:T(8,128)(2,1)} %get-tuple-element.53.refs_11_), calls=%async_computation.1 | async-start | bytes 1310720 | tf_op jit(solution)/shard_map/all_to_all | solution.py:433
  52.8 17.7 %collective-permute-start.6 = (bf16[64,3072]{1,0:T(8,128)(2,1)}, bf16[64,3072]{1,0:T(8,128)(2,1)}, u32[]{:S(2)}, u32[]{:S(2)}) collective-permute-start(bf16[64,3072]{1,0:T(8,128)(2,1)} %collective-permute-done.5.refs_12_.refs_5_), channel_id=1, source_target_pairs={{0,2},{1,3},{2,4},{3,5},{4,6},{5,7},{6,0},{7,1},{8,10},{9,11},{10,... | collective-permute-start | bytes 1179656 | tf_op jit(solution)/shard_map/ppermute | solution.py:388
  90.7 3.5 %collective-permute-start.18 = (bf16[4,64,3072]{2,1,0:T(8,128)(2,1)S(1)}, bf16[4,64,3072]{2,1,0:T(8,128)(2,1)S(1)}, u32[]{:S(2)}, u32[]{:S(2)}) collective-permute-start(bf16[4,64,3072]{2,1,0:T(8,128)(2,1)S(1)} %get-tuple-element.72), channel_id=1, source_target_pairs={{0,1},{1,0},{2,3},{3,2},{4,5},{5,4},{6,7},{7,6},{8,9},{9,8},{10,11... | collective-permute-start | bytes 4718600 | tf_op jit(solution)/shard_map/ppermute | solution.py:394
  90.9 9.1 %collective-permute-start.28 = (bf16[4,64,3072]{2,1,0:T(8,128)(2,1)S(1)}, bf16[4,64,3072]{2,1,0:T(8,128)(2,1)S(1)}, u32[]{:S(2)}, u32[]{:S(2)}) collective-permute-start(bf16[4,64,3072]{2,1,0:T(8,128)(2,1)S(1)} %get-tuple-element.82), channel_id=1, source_target_pairs={{0,1},{1,0},{2,3},{3,2},{4,5},{5,4},{6,7},{7,6},{8,9},{9,8},{10,11... | collective-permute-start | bytes 4718600 | tf_op jit(solution)/shard_map/ppermute | solution.py:394
  96.4 12.0 %collective-permute-start.19 = (bf16[4,64,768]{2,1,0:T(8,128)(2,1)S(1)}, bf16[4,64,768]{2,1,0:T(8,128)(2,1)S(1)}, u32[]{:S(2)}, u32[]{:S(2)}) collective-permute-start(bf16[4,64,768]{2,1,0:T(8,128)(2,1)S(1)} %get-tuple-element.74), channel_id=1, source_target_pairs={{0,8},{8,0},{16,24},{24,16},{1,9},{9,1},{17,25},{25,17},{2,10},{10... | collective-permute-start | bytes 1179656 | tf_op jit(solution)/shard_map/ppermute | solution.py:385
  97.7 20.4 %collective-permute-start.20 = (bf16[4,64,768]{2,1,0:T(8,128)(2,1)S(1)}, bf16[4,64,768]{2,1,0:T(8,128)(2,1)S(1)}, u32[]{:S(2)}, u32[]{:S(2)}) collective-permute-start(bf16[4,64,768]{2,1,0:T(8,128)(2,1)S(1)} %get-tuple-element.75), channel_id=1, source_target_pairs={{0,16},{8,24},{16,0},{24,8},{1,17},{9,25},{17,1},{25,9},{2,18},{10... | collective-permute-start | bytes 1179656 | tf_op jit(solution)/shard_map/ppermute | solution.py:385
  99.0 19.1 %collective-permute-start.21 = (bf16[4,64,768]{2,1,0:T(8,128)(2,1)S(1)}, bf16[4,64,768]{2,1,0:T(8,128)(2,1)S(1)}, u32[]{:S(2)}, u32[]{:S(2)}) collective-permute-start(bf16[4,64,768]{2,1,0:T(8,128)(2,1)S(1)} %get-tuple-element.76), channel_id=1, source_target_pairs={{0,24},{8,16},{16,8},{24,0},{1,25},{9,17},{17,9},{25,1},{2,26},{10... | collective-permute-start | bytes 1179656 | tf_op jit(solution)/shard_map/ppermute | solution.py:385
  100.5 32.0 %collective-permute-start.29 = (bf16[4,64,768]{2,1,0:T(8,128)(2,1)S(1)}, bf16[4,64,768]{2,1,0:T(8,128)(2,1)S(1)}, u32[]{:S(2)}, u32[]{:S(2)}) collective-permute-start(bf16[4,64,768]{2,1,0:T(8,128)(2,1)S(1)} %get-tuple-element.84), channel_id=1, source_target_pairs={{0,8},{8,0},{16,24},{24,16},{1,9},{9,1},{17,25},{25,17},{2,10},{10... | collective-permute-start | bytes 1179656 | tf_op jit(solution)/shard_map/ppermute | solution.py:385
  101.9 36.2 %collective-permute-start.30 = (bf16[4,64,768]{2,1,0:T(8,128)(2,1)S(1)}, bf16[4,64,768]{2,1,0:T(8,128)(2,1)S(1)}, u32[]{:S(2)}, u32[]{:S(2)}) collective-permute-start(bf16[4,64,768]{2,1,0:T(8,128)(2,1)S(1)} %get-tuple-element.85), channel_id=1, source_target_pairs={{0,16},{8,24},{16,0},{24,8},{1,17},{9,25},{17,1},{25,9},{2,18},{10... | collective-permute-start | bytes 1179656 | tf_op jit(solution)/shard_map/ppermute | solution.py:385
  108.4 29.7 %collective-permute-start.31 = (bf16[4,64,768]{2,1,0:T(8,128)(2,1)S(1)}, bf16[4,64,768]{2,1,0:T(8,128)(2,1)S(1)}, u32[]{:S(2)}, u32[]{:S(2)}) collective-permute-start(bf16[4,64,768]{2,1,0:T(8,128)(2,1)S(1)} %get-tuple-element.86), channel_id=1, source_target_pairs={{0,24},{8,16},{16,8},{24,0},{1,25},{9,17},{17,9},{25,1},{2,26},{10... | collective-permute-start | bytes 1179656 | tf_op jit(solution)/shard_map/ppermute | solution.py:385
  118.3 6.1 %collective-permute-start.22 = (bf16[64,768]{1,0:T(8,128)(2,1)S(1)}, bf16[64,768]{1,0:T(8,128)(2,1)S(1)}, u32[]{:S(2)}, u32[]{:S(2)}) collective-permute-start(bf16[64,768]{1,0:T(8,128)(2,1)S(1)} %get-tuple-element.78), channel_id=1, source_target_pairs={{0,2},{1,3},{2,0},{3,1},{4,6},{5,7},{6,4},{7,5},{8,10},{9,11},{10,... | collective-permute-start | bytes 294920 | tf_op jit(solution)/shard_map/ppermute | solution.py:391
  120.7 8.0 %collective-permute-start.23 = (bf16[64,768]{1,0:T(8,128)(2,1)S(1)}, bf16[64,768]{1,0:T(8,128)(2,1)S(1)}, u32[]{:S(2)}, u32[]{:S(2)}) collective-permute-start(bf16[64,768]{1,0:T(8,128)(2,1)S(1)} %get-tuple-element.79), channel_id=1, source_target_pairs={{0,4},{1,5},{2,6},{3,7},{4,0},{5,1},{6,2},{7,3},{8,12},{9,13},{10,... | collective-permute-start | bytes 294920 | tf_op jit(solution)/shard_map/ppermute | solution.py:391
  124.4 6.5 %collective-permute-start.24 = (bf16[64,768]{1,0:T(8,128)(2,1)S(1)}, bf16[64,768]{1,0:T(8,128)(2,1)S(1)}, u32[]{:S(2)}, u32[]{:S(2)}) collective-permute-start(bf16[64,768]{1,0:T(8,128)(2,1)S(1)} %get-tuple-element.80), channel_id=1, source_target_pairs={{0,6},{1,7},{2,4},{3,5},{4,2},{5,3},{6,0},{7,1},{8,14},{9,15},{10,... | collective-permute-start | bytes 294920 | tf_op jit(solution)/shard_map/ppermute | solution.py:391
  130.9 19.3 %collective-permute-start.27 = (f32[64,768]{1,0:T(8,128)S(1)}, f32[64,768]{1,0:T(8,128)S(1)}, u32[]{:S(2)}, u32[]{:S(2)}) collective-permute-start(f32[64,768]{1,0:T(8,128)S(1)} %over_z.2.refs_0_), channel_id=1, source_target_pairs={{0,24},{8,16},{16,8},{24,0},{1,25},{9,17},{17,9},{25,1},{2,26},{10... | collective-permute-start | bytes 589832 | tf_op jit(solution)/shard_map/ppermute | solution.py:385
  138.2 5.8 %collective-permute-start.32 = (bf16[64,768]{1,0:T(8,128)(2,1)S(1)}, bf16[64,768]{1,0:T(8,128)(2,1)S(1)}, u32[]{:S(2)}, u32[]{:S(2)}) collective-permute-start(bf16[64,768]{1,0:T(8,128)(2,1)S(1)} %get-tuple-element.88), channel_id=1, source_target_pairs={{0,2},{1,3},{2,0},{3,1},{4,6},{5,7},{6,4},{7,5},{8,10},{9,11},{10,... | collective-permute-start | bytes 294920 | tf_op jit(solution)/shard_map/ppermute | solution.py:391
  140.7 7.1 %collective-permute-start.33 = (bf16[64,768]{1,0:T(8,128)(2,1)S(1)}, bf16[64,768]{1,0:T(8,128)(2,1)S(1)}, u32[]{:S(2)}, u32[]{:S(2)}) collective-permute-start(bf16[64,768]{1,0:T(8,128)(2,1)S(1)} %get-tuple-element.89), channel_id=1, source_target_pairs={{0,4},{1,5},{2,6},{3,7},{4,0},{5,1},{6,2},{7,3},{8,12},{9,13},{10,... | collective-permute-start | bytes 294920 | tf_op jit(solution)/shard_map/ppermute | solution.py:391
  141.1 6.7 %collective-permute-start.34 = (bf16[64,768]{1,0:T(8,128)(2,1)S(1)}, bf16[64,768]{1,0:T(8,128)(2,1)S(1)}, u32[]{:S(2)}, u32[]{:S(2)}) collective-permute-start(bf16[64,768]{1,0:T(8,128)(2,1)S(1)} %get-tuple-element.90), channel_id=1, source_target_pairs={{0,6},{1,7},{2,4},{3,5},{4,2},{5,3},{6,0},{7,1},{8,14},{9,15},{10,... | collective-permute-start | bytes 294920 | tf_op jit(solution)/shard_map/ppermute | solution.py:391
  143.1 8.4 %collective-permute-start.26 = (f32[64,768]{1,0:T(8,128)S(1)}, f32[64,768]{1,0:T(8,128)S(1)}, u32[]{:S(2)}, u32[]{:S(2)}) collective-permute-start(f32[64,768]{1,0:T(8,128)S(1)} %over_z.2.refs_0_), channel_id=1, source_target_pairs={{0,16},{8,24},{16,0},{24,8},{1,17},{9,25},{17,1},{25,9},{2,18},{10... | collective-permute-start | bytes 589832 | tf_op jit(solution)/shard_map/ppermute | solution.py:385
  144.0 7.5 %collective-permute-start.25 = (f32[64,768]{1,0:T(8,128)S(1)}, f32[64,768]{1,0:T(8,128)S(1)}, u32[]{:S(2)}, u32[]{:S(2)}) collective-permute-start(f32[64,768]{1,0:T(8,128)S(1)} %over_z.2.refs_0_), channel_id=1, source_target_pairs={{0,8},{8,0},{16,24},{24,16},{1,9},{9,1},{17,25},{25,17},{2,10},{10... | collective-permute-start | bytes 589832 | tf_op jit(solution)/shard_map/ppermute | solution.py:385
  147.9 6.7 %collective-permute-start.37 = (f32[64,768]{1,0:T(8,128)S(1)}, f32[64,768]{1,0:T(8,128)S(1)}, u32[]{:S(2)}, u32[]{:S(2)}) collective-permute-start(f32[64,768]{1,0:T(8,128)S(1)} %over_z.3.refs_4_), channel_id=1, source_target_pairs={{0,24},{8,16},{16,8},{24,0},{1,25},{9,17},{17,9},{25,1},{2,26},{10... | collective-permute-start | bytes 589832 | tf_op jit(solution)/shard_map/ppermute | solution.py:385
  149.5 7.1 %collective-permute-start.36 = (f32[64,768]{1,0:T(8,128)S(1)}, f32[64,768]{1,0:T(8,128)S(1)}, u32[]{:S(2)}, u32[]{:S(2)}) collective-permute-start(f32[64,768]{1,0:T(8,128)S(1)} %over_z.3.refs_4_), channel_id=1, source_target_pairs={{0,16},{8,24},{16,0},{24,8},{1,17},{9,25},{17,1},{25,9},{2,18},{10... | collective-permute-start | bytes 589832 | tf_op jit(solution)/shard_map/ppermute | solution.py:385
  150.3 6.4 %collective-permute-start.35 = (f32[64,768]{1,0:T(8,128)S(1)}, f32[64,768]{1,0:T(8,128)S(1)}, u32[]{:S(2)}, u32[]{:S(2)}) collective-permute-start(f32[64,768]{1,0:T(8,128)S(1)} %over_z.3.refs_4_), channel_id=1, source_target_pairs={{0,8},{8,0},{16,24},{24,16},{1,9},{9,1},{17,25},{25,17},{2,10},{10... | collective-permute-start | bytes 589832 | tf_op jit(solution)/shard_map/ppermute | solution.py:385
  (18 other events, 107.6 us)

commit v2 on v1

--- a/solution.py
+++ b/solution.py
@@ -12,7 +12,7 @@
 F32 = jnp.float32
 I32 = jnp.int32
 BLK = 256
-FFN_MB = 50
+FFN_MB = 57
 STUDENT_MB = 44
 VMEM = pl.BlockSpec(memory_space=pltpu.VMEM)
 SMEM = pl.BlockSpec(memory_space=pltpu.SMEM)
@@ -154,8 +154,8 @@
         at += ref.shape[0]
     pairs += list(zip(w_refs, w_bufs))
     copies = [pltpu.make_async_copy(a, b, sem.at[i]) for i, (a, b) in enumerate(pairs)]
-    for c in copies:
-        c.start()
+    for i in [*range(n), n + 2, n + 3, n + 4, n + 5, n, n + 1]:
+        copies[i].start()
     for c in copies[:n]:
         c.wait()
     starts = []
@@ -163,7 +163,7 @@
     for e in e_bufs:
         starts.append(first)
         first += e.shape[1]
-    for k in (0, 2, 1):
+    for k in (1, 2, 0):
         up, down, e = w_bufs[2 * k], w_bufs[2 * k + 1], e_bufs[k]
         width = e.shape[1]
         normed[:, pl.ds(0, width)] = layer_norm(hid[:, pl.ds(starts[k], width)]).astype(BF)

time: 158 us -> 158 us (level)
  waiting for transfers between devices: 64.6 us -> 67.7 us
  starting transfers between devices: 48.4 us -> 46.7 us
    ppermute x19, starting transfers between devices: 25.6 us -> 23.7 us  [swap_t(): return lax.ppermute(value, 'teacher', [(t, t ^ k) for t in range(n_t)])]
    ppermute x19, waiting for transfers between devices: 34.5 us -> 36.2 us  [swap_t(): return lax.ppermute(value, 'teacher', [(t, t ^ k) for t in range(n_t)])]
  transfers between devices with their start and end apart: 40 -> 40, of which waited for: 23 -> 24; matrix products, arithmetic and copies ran while one was open for 0% -> 0% of each run, Pallas kernels for 11% -> 11%
where the time goes in v2:
time: 158 us
  waiting for transfers between devices  67.7 us (43%)
  starting transfers between devices  46.7 us (30%)
  Pallas kernels  38 us (24%)
  local copies, waits for them, and re-layouts  3.86 us (2%)
    ppermute x19, waiting for transfers between devices, swap_t(): return lax.ppermute(value, 'teacher', [(t, t ^ k) for t in range(n_t)])  36.2 us
    ppermute x19, starting transfers between devices, swap_t(): return lax.ppermute(value, 'teacher', [(t, t ^ k) for t in range(n_t)])  23.7 us
    pallas_call x1, Pallas kernels, student_step(): call(functools.partial(student_kernel, (n_t, n_z, rows, out_rows)), 'stud...  14.3 us
    pallas_call x1, Pallas kernels, ffn(): call(functools.partial(ffn_kernel, slice_w, n), 'ffn', [shape((frames, w)...  14.3 us
    ppermute x6, waiting for transfers between devices, swap_z(): return lax.ppermute(value, 'dp', [(d, d ^ 2 * k) for d in range(n_dp)])  11.5 us
    ppermute x3, waiting for transfers between devices, shift_z(): lax.ppermute(value, 'dp', [(d, (d + 2 * k) % n_dp) for d in range(n_dp)])  10.7 us
    ppermute x6, starting transfers between devices, swap_z(): return lax.ppermute(value, 'dp', [(d, d ^ 2 * k) for d in range(n_dp)])  8.7 us
    ppermute x10, waiting for transfers between devices, swap_core(): return lax.ppermute(value, 'dp', [(d, d ^ 1) for d in range(n_dp)])  6.81 us
  transfers between devices with their start and end apart: 40, of which 24 were waited for; matrix products, arithmetic and copies ran while one was open for 0% of the time, Pallas kernels for 11%

profile of v2, /device:TPU:0, one launch (start us, length us, event | category | flops | bytes accessed | tf_op | source)
XLA Modules:
  0.0 157.7 jit_solution(17647274682373844758)
XLA Ops:
  0.6 2.2 %pack.1.after = bf16[512,640]{1,0:T(8,128)(2,1)} custom-call(s32[1,8,8]{2,1,0:T(8,128)} %table.3, bf16[128,512]{1,0:T(8,128)(2,1)} %student.2, bf16[64,3072]{1,0:T(8,128)(2,1)} %w_head.1), custom_call_target="tpu_custom_call" | custom-call | flops 1000000000 | bytes 3000000 | tf_op jit(solution)/shard_map/pack/pallas_call | solution.py:406
  2.9 2.4 %merge.1 = (bf16[64,3072]{1,0:T(8,128)(2,1)}, bf16[128,3072]{1,0:T(8,128)(2,1)}) custom-call(bf16[64,1536]{1,0:T(8,128)(2,1)} %w_in.1, bf16[192,512]{1,0:T(8,128)(2,1)} %w_out.1, bf16[128,1280]{1,0:T(8,128)(2,1)} %whisper.1, bf16[128,768]{1,0:T(8,128)(2,1)} %beats.1, bf16[128,1024]{1,0:T(8,128)(2,1)} %wavlm.1, bf16[512,640]{1,0:T(8,128)(2,1)} %pack.1.after), custom_call_target="tpu_custom_call" | custom-call | flops 1000000000 | bytes 3000000 | tf_op jit(solution)/shard_map/merge/pallas_call | solution.py:412
  5.3 3.0 %collective-permute-start.2 = (bf16[128,3072]{1,0:T(8,128)(2,1)}, bf16[128,3072]{1,0:T(8,128)(2,1)S(1)}, u32[]{:S(2)}, u32[]{:S(2)}) collective-permute-start(bf16[128,3072]{1,0:T(8,128)(2,1)} %get-tuple-element.54.refs_0_), channel_id=1, source_target_pairs={{0,16},{8,24},{16,0},{24,8},{1,17},{9,25},{17,1},{25,9},{2,18},{10... | collective-permute-start | bytes 2359304 | tf_op jit(solution)/shard_map/ppermute | solution.py:385
  9.8 4.9 %all-to-all-start = ((bf16[8,64,640]{2,1,0:T(8,128)(2,1)}), bf16[8,64,640]{2,1,0:T(8,128)(2,1)S(1)}, u32[]{:S(2)}, u32[]{:S(2)}) async-start(bf16[8,64,640]{2,1,0:T(8,128)(2,1)} %bitcast), calls=%async_computation | async-start | bytes 1310720 | tf_op jit(solution)/shard_map/all_to_all | solution.py:410
  14.7 2.0 %collective-permute-start = (bf16[64,3072]{1,0:T(8,128)(2,1)}, bf16[64,3072]{1,0:T(8,128)(2,1)S(1)}, u32[]{:S(2)}, u32[]{:S(2)}) collective-permute-start(bf16[64,3072]{1,0:T(8,128)(2,1)} %get-tuple-element.61.refs_1_), channel_id=1, source_target_pairs={{0,2},{1,3},{2,4},{3,5},{4,6},{5,7},{6,0},{7,1},{8,10},{9,11},{10,... | collective-permute-start | bytes 1179656 | tf_op jit(solution)/shard_map/ppermute | solution.py:388
  16.7 9.4 %collective-permute-done.2.from_y.refs_2_ = bf16[128,3072]{1,0:T(8,128)(2,1)S(1)} collective-permute-done((bf16[128,3072]{1,0:T(8,128)(2,1)}, bf16[128,3072]{1,0:T(8,128)(2,1)S(1)}, u32[]{:S(2)}, u32[]{:S(2)}) %collective-permute-start.2) | collective-permute-done | bytes 786464 | tf_op jit(solution)/shard_map/ppermute | solution.py:385
  27.9 1.6 collective-permute-start.3
  30.0 8.8 %collective-permute-done.refs_3_ = bf16[64,3072]{1,0:T(8,128)(2,1)S(1)} collective-permute-done((bf16[64,3072]{1,0:T(8,128)(2,1)}, bf16[64,3072]{1,0:T(8,128)(2,1)S(1)}, u32[]{:S(2)}, u32[]{:S(2)}) %collective-permute-start) | collective-permute-done | bytes 393248 | tf_op jit(solution)/shard_map/ppermute | solution.py:388
  41.3 1.7 %unpack.1 = (bf16[4,128,640]{2,1,0:T(8,128)(2,1)}, bf16[512,384]{1,0:T(8,128)(2,1)S(1)}) custom-call(s32[1,8,8]{2,1,0:T(8,128)S(1)} %copy-done.7, s32[1]{0:T(128)S(6)} %copy.18.clip_len, bf16[512,640]{1,0:T(8,128)(2,1)S(1)} %bitcast.2), custom_call_target="tpu_custom_call" | custom-call | flops 1000000000 | bytes 3000000 | tf_op jit(solution)/shard_map/unpack/pallas_call | solution.py:429
  46.5 3.5 %all-to-all-start.1 = ((bf16[4,128,640]{2,1,0:T(8,128)(2,1)}), bf16[4,128,640]{2,1,0:T(8,128)(2,1)S(1)}, u32[]{:S(2)}, u32[]{:S(2)}) async-start(bf16[4,128,640]{2,1,0:T(8,128)(2,1)} %get-tuple-element.53.refs_11_), calls=%async_computation.1 | async-start | bytes 1310720 | tf_op jit(solution)/shard_map/all_to_all | solution.py:433
  50.0 1.9 %collective-permute-done.5.refs_12_.refs_5_ = bf16[64,3072]{1,0:T(8,128)(2,1)S(1)} collective-permute-done((bf16[64,3072]{1,0:T(8,128)(2,1)S(1)}, bf16[64,3072]{1,0:T(8,128)(2,1)S(1)}, u32[]{:S(2)}, u32[]{:S(2)}) %collective-permute-start.5) | collective-permute-done | bytes 393248 | tf_op jit(solution)/shard_map/ppermute | solution.py:388
  52.7 14.3 %ffn.1 = (f32[512,1280]{1,0:T(8,128)}, f32[512,768]{1,0:T(8,128)}, f32[512,1024]{1,0:T(8,128)}) custom-call(bf16[128,3072]{1,0:T(8,128)(2,1)} %get-tuple-element.54.refs_0_, bf16[128,3072]{1,0:T(8,128)(2,1)} %copy-done.3, bf16[128,3072]{1,0:T(8,128)(2,1)} %copy-done.2, bf16[64,3072]{1,0:T(8,128)(2,1)} %copy-done.8, bf16[64,3072]{1,0:T(8,128)(2,1)} %copy-done.9, ...), custom_call_target="tpu_custom_call" | custom-call | flops 12999999488 | bytes 39000000 | tf_op jit(solution)/shard_map/ffn/pallas_call | solution.py:187
  67.0 2.5 %all-to-all-done.1.refs_0_ = bf16[4,128,640]{2,1,0:T(8,128)(2,1)S(1)} async-done(((bf16[4,128,640]{2,1,0:T(8,128)(2,1)}), bf16[4,128,640]{2,1,0:T(8,128)(2,1)S(1)}, u32[]{:S(2)}, u32[]{:S(2)}) %all-to-all-start.1) | async-done | bytes 655392 | tf_op jit(solution)/shard_map/all_to_all | solution.py:433
  76.2 14.3 %student.3 = (f32[4,64,3072]{2,1,0:T(8,128)}, bf16[4,64,3072]{2,1,0:T(8,128)(2,1)S(1)}, f32[4,64,3072]{2,1,0:T(8,128)}, bf16[4,64,3072]{2,1,0:T(8,128)(2,1)S(1)}) custom-call(bf16[4,128,640]{2,1,0:T(8,128)(2,1)S(1)} %all-to-all-done.1.refs_0_, bf16[64,3072]{1,0:T(8,128)(2,1)S(1)} %copy-done.4, bf16[64,3072]{1,0:T(8,128)(2,1)S(1)} %collective-permute-done.10.refs_2_, ...), custom_call_target="tpu_custom_call" | custom-call | flops 14000000000 | bytes 42000000 | tf_op jit(solution)/shard_map/student/pallas_call | solution.py:296
  91.1 2.9 %collective-permute-done.18.recv = bf16[4,64,3072]{2,1,0:T(8,128)(2,1)S(1)} collective-permute-done((bf16[4,64,3072]{2,1,0:T(8,128)(2,1)S(1)}, bf16[4,64,3072]{2,1,0:T(8,128)(2,1)S(1)}, u32[]{:S(2)}, u32[]{:S(2)}) %collective-permute-start.18) | collective-permute-done | bytes 1572896 | tf_op jit(solution)/shard_map/ppermute | solution.py:394
  94.0 1.9 %copy-done.1 = f32[4,64,3072]{2,1,0:T(8,128)S(1)} copy-done((f32[4,64,3072]{2,1,0:T(8,128)S(1)}, f32[4,64,3072]{2,1,0:T(8,128)}, u32[]{:S(2)}) %copy-start.1) | copy-done | bytes 3145752
  98.0 1.7 %collective-permute-start.21 = (bf16[4,64,768]{2,1,0:T(8,128)(2,1)S(1)}, bf16[4,64,768]{2,1,0:T(8,128)(2,1)S(1)}, u32[]{:S(2)}, u32[]{:S(2)}) collective-permute-start(bf16[4,64,768]{2,1,0:T(8,128)(2,1)S(1)} %get-tuple-element.76), channel_id=1, source_target_pairs={{0,24},{8,16},{16,8},{24,0},{1,25},{9,17},{17,9},{25,1},{2,26},{10... | collective-permute-start | bytes 1179656 | tf_op jit(solution)/shard_map/ppermute | solution.py:385
  102.2 6.0 %collective-permute-done.19.refs_0_ = bf16[4,64,768]{2,1,0:T(8,128)(2,1)S(1)} collective-permute-done((bf16[4,64,768]{2,1,0:T(8,128)(2,1)S(1)}, bf16[4,64,768]{2,1,0:T(8,128)(2,1)S(1)}, u32[]{:S(2)}, u32[]{:S(2)}) %collective-permute-start.19) | collective-permute-done | bytes 393248 | tf_op jit(solution)/shard_map/ppermute | solution.py:385
  109.4 8.5 %collective-permute-done.20.refs_1_ = bf16[4,64,768]{2,1,0:T(8,128)(2,1)S(1)} collective-permute-done((bf16[4,64,768]{2,1,0:T(8,128)(2,1)S(1)}, bf16[4,64,768]{2,1,0:T(8,128)(2,1)S(1)}, u32[]{:S(2)}, u32[]{:S(2)}) %collective-permute-start.20) | collective-permute-done | bytes 393248 | tf_op jit(solution)/shard_map/ppermute | solution.py:385
  118.1 2.4 %collective-permute-start.22 = (bf16[64,768]{1,0:T(8,128)(2,1)S(1)}, bf16[64,768]{1,0:T(8,128)(2,1)S(1)}, u32[]{:S(2)}, u32[]{:S(2)}) collective-permute-start(bf16[64,768]{1,0:T(8,128)(2,1)S(1)} %get-tuple-element.78), channel_id=1, source_target_pairs={{0,2},{1,3},{2,0},{3,1},{4,6},{5,7},{6,4},{7,5},{8,10},{9,11},{10,... | collective-permute-start | bytes 294920 | tf_op jit(solution)/shard_map/ppermute | solution.py:391
  121.0 3.2 %collective-permute-done.22.refs_0_ = bf16[64,768]{1,0:T(8,128)(2,1)S(1)} collective-permute-done((bf16[64,768]{1,0:T(8,128)(2,1)S(1)}, bf16[64,768]{1,0:T(8,128)(2,1)S(1)}, u32[]{:S(2)}, u32[]{:S(2)}) %collective-permute-start.22) | collective-permute-done | bytes 98336 | tf_op jit(solution)/shard_map/ppermute | solution.py:391
  125.1 3.5 %collective-permute-done.23.refs_1_ = bf16[64,768]{1,0:T(8,128)(2,1)S(1)} collective-permute-done((bf16[64,768]{1,0:T(8,128)(2,1)S(1)}, bf16[64,768]{1,0:T(8,128)(2,1)S(1)}, u32[]{:S(2)}, u32[]{:S(2)}) %collective-permute-start.23) | collective-permute-done | bytes 98336 | tf_op jit(solution)/shard_map/ppermute | solution.py:391
  128.6 2.1 %collective-permute-done.24.refs_2_ = bf16[64,768]{1,0:T(8,128)(2,1)S(1)} collective-permute-done((bf16[64,768]{1,0:T(8,128)(2,1)S(1)}, bf16[64,768]{1,0:T(8,128)(2,1)S(1)}, u32[]{:S(2)}, u32[]{:S(2)}) %collective-permute-start.24) | collective-permute-done | bytes 98336 | tf_op jit(solution)/shard_map/ppermute | solution.py:391
  130.8 1.6 collective-permute-start.27
  132.3 5.6 %collective-permute-done.30.refs_1_ = bf16[4,64,768]{2,1,0:T(8,128)(2,1)S(1)} collective-permute-done((bf16[4,64,768]{2,1,0:T(8,128)(2,1)S(1)}, bf16[4,64,768]{2,1,0:T(8,128)(2,1)S(1)}, u32[]{:S(2)}, u32[]{:S(2)}) %collective-permute-start.30) | collective-permute-done | bytes 393248 | tf_op jit(solution)/shard_map/ppermute | solution.py:385
  138.1 2.4 %collective-permute-start.32 = (bf16[64,768]{1,0:T(8,128)(2,1)S(1)}, bf16[64,768]{1,0:T(8,128)(2,1)S(1)}, u32[]{:S(2)}, u32[]{:S(2)}) collective-permute-start(bf16[64,768]{1,0:T(8,128)(2,1)S(1)} %get-tuple-element.88), channel_id=1, source_target_pairs={{0,2},{1,3},{2,0},{3,1},{4,6},{5,7},{6,4},{7,5},{8,10},{9,11},{10,... | collective-permute-start | bytes 294920 | tf_op jit(solution)/shard_map/ppermute | solution.py:391
  141.0 2.0 %collective-permute-start.34 = (bf16[64,768]{1,0:T(8,128)(2,1)S(1)}, bf16[64,768]{1,0:T(8,128)(2,1)S(1)}, u32[]{:S(2)}, u32[]{:S(2)}) collective-permute-start(bf16[64,768]{1,0:T(8,128)(2,1)S(1)} %get-tuple-element.90), channel_id=1, source_target_pairs={{0,6},{1,7},{2,4},{3,5},{4,2},{5,3},{6,0},{7,1},{8,14},{9,15},{10,... | collective-permute-start | bytes 294920 | tf_op jit(solution)/shard_map/ppermute | solution.py:391
  143.1 1.9 %collective-permute-start.25 = (f32[64,768]{1,0:T(8,128)S(1)}, f32[64,768]{1,0:T(8,128)S(1)}, u32[]{:S(2)}, u32[]{:S(2)}) collective-permute-start(f32[64,768]{1,0:T(8,128)S(1)} %over_z.2.refs_0_), channel_id=1, source_target_pairs={{0,8},{8,0},{16,24},{24,16},{1,9},{9,1},{17,25},{25,17},{2,10},{10... | collective-permute-start | bytes 589832 | tf_op jit(solution)/shard_map/ppermute | solution.py:385
  145.0 2.6 %collective-permute-done.33.refs_1_ = bf16[64,768]{1,0:T(8,128)(2,1)S(1)} collective-permute-done((bf16[64,768]{1,0:T(8,128)(2,1)S(1)}, bf16[64,768]{1,0:T(8,128)(2,1)S(1)}, u32[]{:S(2)}, u32[]{:S(2)}) %collective-permute-start.33) | collective-permute-done | bytes 98336 | tf_op jit(solution)/shard_map/ppermute | solution.py:391
  147.7 1.6 %collective-permute-start.37 = (f32[64,768]{1,0:T(8,128)S(1)}, f32[64,768]{1,0:T(8,128)S(1)}, u32[]{:S(2)}, u32[]{:S(2)}) collective-permute-start(f32[64,768]{1,0:T(8,128)S(1)} %over_z.3.refs_4_), channel_id=1, source_target_pairs={{0,24},{8,16},{16,8},{24,0},{1,25},{9,17},{17,9},{25,1},{2,26},{10... | collective-permute-start | bytes 589832 | tf_op jit(solution)/shard_map/ppermute | solution.py:385
  151.4 3.0 %collective-permute-done.37.refs_7_ = f32[64,768]{1,0:T(8,128)S(1)} collective-permute-done((f32[64,768]{1,0:T(8,128)S(1)}, f32[64,768]{1,0:T(8,128)S(1)}, u32[]{:S(2)}, u32[]{:S(2)}) %collective-permute-start.37) | collective-permute-done | bytes 196640 | tf_op jit(solution)/shard_map/ppermute | solution.py:385
  154.4 2.0 %collective-permute-done.36.refs_6_ = f32[64,768]{1,0:T(8,128)S(1)} collective-permute-done((f32[64,768]{1,0:T(8,128)S(1)}, f32[64,768]{1,0:T(8,128)S(1)}, u32[]{:S(2)}, u32[]{:S(2)}) %collective-permute-start.36) | collective-permute-done | bytes 196640 | tf_op jit(solution)/shard_map/ppermute | solution.py:385
  (81 shorter events, 28.7 us)
Async XLA Ops:
  5.3 20.8 %collective-permute-start.2 = (bf16[128,3072]{1,0:T(8,128)(2,1)}, bf16[128,3072]{1,0:T(8,128)(2,1)S(1)}, u32[]{:S(2)}, u32[]{:S(2)}) collective-permute-start(bf16[128,3072]{1,0:T(8,128)(2,1)} %get-tuple-element.54.refs_0_), channel_id=1, source_target_pairs={{0,16},{8,24},{16,0},{24,8},{1,17},{9,25},{17,1},{25,9},{2,18},{10... | collective-permute-start | bytes 2359304 | tf_op jit(solution)/shard_map/ppermute | solution.py:385
  8.3 19.2 %collective-permute-start.1 = (bf16[128,3072]{1,0:T(8,128)(2,1)}, bf16[128,3072]{1,0:T(8,128)(2,1)S(1)}, u32[]{:S(2)}, u32[]{:S(2)}) collective-permute-start(bf16[128,3072]{1,0:T(8,128)(2,1)} %get-tuple-element.54.refs_0_), channel_id=1, source_target_pairs={{0,8},{8,0},{16,24},{24,16},{1,9},{9,1},{17,25},{25,17},{2,10},{10... | collective-permute-start | bytes 2359304 | tf_op jit(solution)/shard_map/ppermute | solution.py:385
  9.8 31.5 %all-to-all-start = ((bf16[8,64,640]{2,1,0:T(8,128)(2,1)}), bf16[8,64,640]{2,1,0:T(8,128)(2,1)S(1)}, u32[]{:S(2)}, u32[]{:S(2)}) async-start(bf16[8,64,640]{2,1,0:T(8,128)(2,1)} %bitcast), calls=%async_computation | async-start | bytes 1310720 | tf_op jit(solution)/shard_map/all_to_all | solution.py:410
  14.7 24.1 %collective-permute-start = (bf16[64,3072]{1,0:T(8,128)(2,1)}, bf16[64,3072]{1,0:T(8,128)(2,1)S(1)}, u32[]{:S(2)}, u32[]{:S(2)}) collective-permute-start(bf16[64,3072]{1,0:T(8,128)(2,1)} %get-tuple-element.61.refs_1_), channel_id=1, source_target_pairs={{0,2},{1,3},{2,4},{3,5},{4,6},{5,7},{6,0},{7,1},{8,10},{9,11},{10,... | collective-permute-start | bytes 1179656 | tf_op jit(solution)/shard_map/ppermute | solution.py:388
  27.9 10.9 %collective-permute-start.3 = (bf16[64,3072]{1,0:T(8,128)(2,1)S(1)}, bf16[64,3072]{1,0:T(8,128)(2,1)S(1)}, u32[]{:S(2)}, u32[]{:S(2)}) collective-permute-start(bf16[64,3072]{1,0:T(8,128)(2,1)S(1)} %get-tuple-element.49), channel_id=1, source_target_pairs={{0,8},{8,0},{16,24},{24,16},{1,9},{9,1},{17,25},{25,17},{2,10},{10... | collective-permute-start | bytes 1179656 | tf_op jit(solution)/shard_map/ppermute | solution.py:385
  29.5 10.1 %collective-permute-start.4 = (bf16[64,3072]{1,0:T(8,128)(2,1)S(1)}, bf16[64,3072]{1,0:T(8,128)(2,1)S(1)}, u32[]{:S(2)}, u32[]{:S(2)}) collective-permute-start(bf16[64,3072]{1,0:T(8,128)(2,1)S(1)} %get-tuple-element.50), channel_id=1, source_target_pairs={{0,16},{8,24},{16,0},{24,8},{1,17},{9,25},{17,1},{25,9},{2,18},{10... | collective-permute-start | bytes 1179656 | tf_op jit(solution)/shard_map/ppermute | solution.py:385
  39.5 12.4 %collective-permute-start.5 = (bf16[64,3072]{1,0:T(8,128)(2,1)S(1)}, bf16[64,3072]{1,0:T(8,128)(2,1)S(1)}, u32[]{:S(2)}, u32[]{:S(2)}) collective-permute-start(bf16[64,3072]{1,0:T(8,128)(2,1)S(1)} %collective-permute-done.refs_3_), channel_id=1, source_target_pairs={{0,2},{1,3},{2,4},{3,5},{4,6},{5,7},{6,0},{7,1},{8,10},{9,11},{10,... | collective-permute-start | bytes 1179656 | tf_op jit(solution)/shard_map/ppermute | solution.py:388
  43.0 24.0 %collective-permute-start.9 = (bf16[512,384]{1,0:T(8,128)(2,1)S(1)}, bf16[512,384]{1,0:T(8,128)(2,1)S(1)}, u32[]{:S(2)}, u32[]{:S(2)}) collective-permute-start(bf16[512,384]{1,0:T(8,128)(2,1)S(1)} %get-tuple-element.65.refs_9_), channel_id=1, source_target_pairs={{0,24},{8,16},{16,8},{24,0},{1,25},{9,17},{17,9},{25,1},{2,26},{10... | collective-permute-start | bytes 1179656 | tf_op jit(solution)/shard_map/ppermute | solution.py:385
  43.9 23.1 %collective-permute-start.8 = (bf16[512,384]{1,0:T(8,128)(2,1)S(1)}, bf16[512,384]{1,0:T(8,128)(2,1)S(1)}, u32[]{:S(2)}, u32[]{:S(2)}) collective-permute-start(bf16[512,384]{1,0:T(8,128)(2,1)S(1)} %get-tuple-element.65.refs_9_), channel_id=1, source_target_pairs={{0,16},{8,24},{16,0},{24,8},{1,17},{9,25},{17,1},{25,9},{2,18},{10... | collective-permute-start | bytes 1179656 | tf_op jit(solution)/shard_map/ppermute | solution.py:385
  45.3 21.7 %collective-permute-start.7 = (bf16[512,384]{1,0:T(8,128)(2,1)S(1)}, bf16[512,384]{1,0:T(8,128)(2,1)S(1)}, u32[]{:S(2)}, u32[]{:S(2)}) collective-permute-start(bf16[512,384]{1,0:T(8,128)(2,1)S(1)} %get-tuple-element.65.refs_9_), channel_id=1, source_target_pairs={{0,8},{8,0},{16,24},{24,16},{1,9},{9,1},{17,25},{25,17},{2,10},{10... | collective-permute-start | bytes 1179656 | tf_op jit(solution)/shard_map/ppermute | solution.py:385
  46.5 23.0 %all-to-all-start.1 = ((bf16[4,128,640]{2,1,0:T(8,128)(2,1)}), bf16[4,128,640]{2,1,0:T(8,128)(2,1)S(1)}, u32[]{:S(2)}, u32[]{:S(2)}) async-start(bf16[4,128,640]{2,1,0:T(8,128)(2,1)} %get-tuple-element.53.refs_11_), calls=%async_computation.1 | async-start | bytes 1310720 | tf_op jit(solution)/shard_map/all_to_all | solution.py:433
  51.9 17.6 %collective-permute-start.6 = (bf16[64,3072]{1,0:T(8,128)(2,1)S(1)}, bf16[64,3072]{1,0:T(8,128)(2,1)}, u32[]{:S(2)}, u32[]{:S(2)}) collective-permute-start(bf16[64,3072]{1,0:T(8,128)(2,1)S(1)} %collective-permute-done.5.refs_12_.refs_5_), channel_id=1, source_target_pairs={{0,2},{1,3},{2,4},{3,5},{4,6},{5,7},{6,0},{7,1},{8,10},{9,11},{10,... | collective-permute-start | bytes 1179656 | tf_op jit(solution)/shard_map/ppermute | solution.py:388
  70.1 3.8 %collective-permute-start.13 = (bf16[64,3072]{1,0:T(8,128)(2,1)}, bf16[64,3072]{1,0:T(8,128)(2,1)S(1)}, u32[]{:S(2)}, u32[]{:S(2)}) collective-permute-start(bf16[64,3072]{1,0:T(8,128)(2,1)} %collective-permute-done.6.refs_7_), channel_id=1, source_target_pairs={{0,1},{1,0},{2,3},{3,2},{4,5},{5,4},{6,7},{7,6},{8,9},{9,8},{10,11... | collective-permute-start | bytes 1179656 | tf_op jit(solution)/shard_map/ppermute | solution.py:394
  90.7 9.1 %collective-permute-start.28 = (bf16[4,64,3072]{2,1,0:T(8,128)(2,1)S(1)}, bf16[4,64,3072]{2,1,0:T(8,128)(2,1)S(1)}, u32[]{:S(2)}, u32[]{:S(2)}) collective-permute-start(bf16[4,64,3072]{2,1,0:T(8,128)(2,1)S(1)} %get-tuple-element.82), channel_id=1, source_target_pairs={{0,1},{1,0},{2,3},{3,2},{4,5},{5,4},{6,7},{7,6},{8,9},{9,8},{10,11... | collective-permute-start | bytes 4718600 | tf_op jit(solution)/shard_map/ppermute | solution.py:394
  96.2 12.0 %collective-permute-start.19 = (bf16[4,64,768]{2,1,0:T(8,128)(2,1)S(1)}, bf16[4,64,768]{2,1,0:T(8,128)(2,1)S(1)}, u32[]{:S(2)}, u32[]{:S(2)}) collective-permute-start(bf16[4,64,768]{2,1,0:T(8,128)(2,1)S(1)} %get-tuple-element.74), channel_id=1, source_target_pairs={{0,8},{8,0},{16,24},{24,16},{1,9},{9,1},{17,25},{25,17},{2,10},{10... | collective-permute-start | bytes 1179656 | tf_op jit(solution)/shard_map/ppermute | solution.py:385
  97.5 20.4 %collective-permute-start.20 = (bf16[4,64,768]{2,1,0:T(8,128)(2,1)S(1)}, bf16[4,64,768]{2,1,0:T(8,128)(2,1)S(1)}, u32[]{:S(2)}, u32[]{:S(2)}) collective-permute-start(bf16[4,64,768]{2,1,0:T(8,128)(2,1)S(1)} %get-tuple-element.75), channel_id=1, source_target_pairs={{0,16},{8,24},{16,0},{24,8},{1,17},{9,25},{17,1},{25,9},{2,18},{10... | collective-permute-start | bytes 1179656 | tf_op jit(solution)/shard_map/ppermute | solution.py:385
  98.0 19.9 %collective-permute-start.21 = (bf16[4,64,768]{2,1,0:T(8,128)(2,1)S(1)}, bf16[4,64,768]{2,1,0:T(8,128)(2,1)S(1)}, u32[]{:S(2)}, u32[]{:S(2)}) collective-permute-start(bf16[4,64,768]{2,1,0:T(8,128)(2,1)S(1)} %get-tuple-element.76), channel_id=1, source_target_pairs={{0,24},{8,16},{16,8},{24,0},{1,25},{9,17},{17,9},{25,1},{2,26},{10... | collective-permute-start | bytes 1179656 | tf_op jit(solution)/shard_map/ppermute | solution.py:385
  100.4 32.0 %collective-permute-start.29 = (bf16[4,64,768]{2,1,0:T(8,128)(2,1)S(1)}, bf16[4,64,768]{2,1,0:T(8,128)(2,1)S(1)}, u32[]{:S(2)}, u32[]{:S(2)}) collective-permute-start(bf16[4,64,768]{2,1,0:T(8,128)(2,1)S(1)} %get-tuple-element.84), channel_id=1, source_target_pairs={{0,8},{8,0},{16,24},{24,16},{1,9},{9,1},{17,25},{25,17},{2,10},{10... | collective-permute-start | bytes 1179656 | tf_op jit(solution)/shard_map/ppermute | solution.py:385
  101.7 36.2 %collective-permute-start.30 = (bf16[4,64,768]{2,1,0:T(8,128)(2,1)S(1)}, bf16[4,64,768]{2,1,0:T(8,128)(2,1)S(1)}, u32[]{:S(2)}, u32[]{:S(2)}) collective-permute-start(bf16[4,64,768]{2,1,0:T(8,128)(2,1)S(1)} %get-tuple-element.85), channel_id=1, source_target_pairs={{0,16},{8,24},{16,0},{24,8},{1,17},{9,25},{17,1},{25,9},{2,18},{10... | collective-permute-start | bytes 1179656 | tf_op jit(solution)/shard_map/ppermute | solution.py:385
  108.2 29.7 %collective-permute-start.31 = (bf16[4,64,768]{2,1,0:T(8,128)(2,1)S(1)}, bf16[4,64,768]{2,1,0:T(8,128)(2,1)S(1)}, u32[]{:S(2)}, u32[]{:S(2)}) collective-permute-start(bf16[4,64,768]{2,1,0:T(8,128)(2,1)S(1)} %get-tuple-element.86), channel_id=1, source_target_pairs={{0,24},{8,16},{16,8},{24,0},{1,25},{9,17},{17,9},{25,1},{2,26},{10... | collective-permute-start | bytes 1179656 | tf_op jit(solution)/shard_map/ppermute | solution.py:385
  118.1 6.1 %collective-permute-start.22 = (bf16[64,768]{1,0:T(8,128)(2,1)S(1)}, bf16[64,768]{1,0:T(8,128)(2,1)S(1)}, u32[]{:S(2)}, u32[]{:S(2)}) collective-permute-start(bf16[64,768]{1,0:T(8,128)(2,1)S(1)} %get-tuple-element.78), channel_id=1, source_target_pairs={{0,2},{1,3},{2,0},{3,1},{4,6},{5,7},{6,4},{7,5},{8,10},{9,11},{10,... | collective-permute-start | bytes 294920 | tf_op jit(solution)/shard_map/ppermute | solution.py:391
  120.6 8.0 %collective-permute-start.23 = (bf16[64,768]{1,0:T(8,128)(2,1)S(1)}, bf16[64,768]{1,0:T(8,128)(2,1)S(1)}, u32[]{:S(2)}, u32[]{:S(2)}) collective-permute-start(bf16[64,768]{1,0:T(8,128)(2,1)S(1)} %get-tuple-element.79), channel_id=1, source_target_pairs={{0,4},{1,5},{2,6},{3,7},{4,0},{5,1},{6,2},{7,3},{8,12},{9,13},{10,... | collective-permute-start | bytes 294920 | tf_op jit(solution)/shard_map/ppermute | solution.py:391
  124.2 6.5 %collective-permute-start.24 = (bf16[64,768]{1,0:T(8,128)(2,1)S(1)}, bf16[64,768]{1,0:T(8,128)(2,1)S(1)}, u32[]{:S(2)}, u32[]{:S(2)}) collective-permute-start(bf16[64,768]{1,0:T(8,128)(2,1)S(1)} %get-tuple-element.80), channel_id=1, source_target_pairs={{0,6},{1,7},{2,4},{3,5},{4,2},{5,3},{6,0},{7,1},{8,14},{9,15},{10,... | collective-permute-start | bytes 294920 | tf_op jit(solution)/shard_map/ppermute | solution.py:391
  130.8 19.2 %collective-permute-start.27 = (f32[64,768]{1,0:T(8,128)S(1)}, f32[64,768]{1,0:T(8,128)S(1)}, u32[]{:S(2)}, u32[]{:S(2)}) collective-permute-start(f32[64,768]{1,0:T(8,128)S(1)} %over_z.2.refs_0_), channel_id=1, source_target_pairs={{0,24},{8,16},{16,8},{24,0},{1,25},{9,17},{17,9},{25,1},{2,26},{10... | collective-permute-start | bytes 589832 | tf_op jit(solution)/shard_map/ppermute | solution.py:385
  138.1 5.0 %collective-permute-start.32 = (bf16[64,768]{1,0:T(8,128)(2,1)S(1)}, bf16[64,768]{1,0:T(8,128)(2,1)S(1)}, u32[]{:S(2)}, u32[]{:S(2)}) collective-permute-start(bf16[64,768]{1,0:T(8,128)(2,1)S(1)} %get-tuple-element.88), channel_id=1, source_target_pairs={{0,2},{1,3},{2,0},{3,1},{4,6},{5,7},{6,4},{7,5},{8,10},{9,11},{10,... | collective-permute-start | bytes 294920 | tf_op jit(solution)/shard_map/ppermute | solution.py:391
  140.5 7.1 %collective-permute-start.33 = (bf16[64,768]{1,0:T(8,128)(2,1)S(1)}, bf16[64,768]{1,0:T(8,128)(2,1)S(1)}, u32[]{:S(2)}, u32[]{:S(2)}) collective-permute-start(bf16[64,768]{1,0:T(8,128)(2,1)S(1)} %get-tuple-element.89), channel_id=1, source_target_pairs={{0,4},{1,5},{2,6},{3,7},{4,0},{5,1},{6,2},{7,3},{8,12},{9,13},{10,... | collective-permute-start | bytes 294920 | tf_op jit(solution)/shard_map/ppermute | solution.py:391
  141.0 6.7 %collective-permute-start.34 = (bf16[64,768]{1,0:T(8,128)(2,1)S(1)}, bf16[64,768]{1,0:T(8,128)(2,1)S(1)}, u32[]{:S(2)}, u32[]{:S(2)}) collective-permute-start(bf16[64,768]{1,0:T(8,128)(2,1)S(1)} %get-tuple-element.90), channel_id=1, source_target_pairs={{0,6},{1,7},{2,4},{3,5},{4,2},{5,3},{6,0},{7,1},{8,14},{9,15},{10,... | collective-permute-start | bytes 294920 | tf_op jit(solution)/shard_map/ppermute | solution.py:391
  143.0 8.4 %collective-permute-start.26 = (f32[64,768]{1,0:T(8,128)S(1)}, f32[64,768]{1,0:T(8,128)S(1)}, u32[]{:S(2)}, u32[]{:S(2)}) collective-permute-start(f32[64,768]{1,0:T(8,128)S(1)} %over_z.2.refs_0_), channel_id=1, source_target_pairs={{0,16},{8,24},{16,0},{24,8},{1,17},{9,25},{17,1},{25,9},{2,18},{10... | collective-permute-start | bytes 589832 | tf_op jit(solution)/shard_map/ppermute | solution.py:385
  143.1 8.3 %collective-permute-start.25 = (f32[64,768]{1,0:T(8,128)S(1)}, f32[64,768]{1,0:T(8,128)S(1)}, u32[]{:S(2)}, u32[]{:S(2)}) collective-permute-start(f32[64,768]{1,0:T(8,128)S(1)} %over_z.2.refs_0_), channel_id=1, source_target_pairs={{0,8},{8,0},{16,24},{24,16},{1,9},{9,1},{17,25},{25,17},{2,10},{10... | collective-permute-start | bytes 589832 | tf_op jit(solution)/shard_map/ppermute | solution.py:385
  147.7 6.7 %collective-permute-start.37 = (f32[64,768]{1,0:T(8,128)S(1)}, f32[64,768]{1,0:T(8,128)S(1)}, u32[]{:S(2)}, u32[]{:S(2)}) collective-permute-start(f32[64,768]{1,0:T(8,128)S(1)} %over_z.3.refs_4_), channel_id=1, source_target_pairs={{0,24},{8,16},{16,8},{24,0},{1,25},{9,17},{17,9},{25,1},{2,26},{10... | collective-permute-start | bytes 589832 | tf_op jit(solution)/shard_map/ppermute | solution.py:385
  149.3 7.1 %collective-permute-start.36 = (f32[64,768]{1,0:T(8,128)S(1)}, f32[64,768]{1,0:T(8,128)S(1)}, u32[]{:S(2)}, u32[]{:S(2)}) collective-permute-start(f32[64,768]{1,0:T(8,128)S(1)} %over_z.3.refs_4_), channel_id=1, source_target_pairs={{0,16},{8,24},{16,0},{24,8},{1,17},{9,25},{17,1},{25,9},{2,18},{10... | collective-permute-start | bytes 589832 | tf_op jit(solution)/shard_map/ppermute | solution.py:385
  150.0 6.5 %collective-permute-start.35 = (f32[64,768]{1,0:T(8,128)S(1)}, f32[64,768]{1,0:T(8,128)S(1)}, u32[]{:S(2)}, u32[]{:S(2)}) collective-permute-start(f32[64,768]{1,0:T(8,128)S(1)} %over_z.3.refs_4_), channel_id=1, source_target_pairs={{0,8},{8,0},{16,24},{24,16},{1,9},{9,1},{17,25},{25,17},{2,10},{10... | collective-permute-start | bytes 589832 | tf_op jit(solution)/shard_map/ppermute | solution.py:385
  (18 other events, 110.2 us)
